TPU v7x, 32 devices: a whole 2x2x4 slice. The times are simulated.
32 devices in a mesh: groups: 2 (over y), aux: 4 (over z), pts: 2 (over x), rep: 2 (over core).
Axes of the slice: x: 2, y: 2, z: 4, core: 2. Of those that a mesh axis runs over, the one named last changes fastest.
Arguments:
- density_slab: bfloat16 [32, 1024, 1024], P('groups', 'aux', 'rep'), parts along dimension 0, may hold values from -0.005859375 to 0.005859375
- orbitals: bfloat16 [2048, 8192], P(('groups', 'rep'), 'pts'), parts along dimension 0, may hold values from -6 to 6
Outputs:
- rhs_share: float32 [16384, 8192], P(('groups', 'pts'), ('aux', 'rep')), parts along dimension 0
There are 2 independent parts, one for each index of `groups`. A program takes and returns all parts, laid end to end along the dimension named above; each array names one. Nothing has to cross between parts.
All inputs are finite; a program needn't handle non-finite values.
Results may differ from a plain program's by a relative error of at most 0.0003.
Values may be sent and summed in bfloat16 or wider, within the bound.
No kernel may reach another device: no remote copies, remote signals or barrier semaphores. Data moves between devices by JAX's collectives and lax.ppermute only.
A program may use at most 64 MiB of HBM per device.

v0:
```python
import jax
import jax.numpy as jnp
from jax import lax
from jax.sharding import PartitionSpec as P


def spread_points(own_weights):
    return lax.all_gather(own_weights, "pts", axis=1, tiled=True)


def all_rows(orbitals):
    return lax.all_gather(orbitals, "rep", axis=0, tiled=True)


def per_device(density_slab, orbitals):
    aux_index = lax.axis_index("aux")
    rep_index = lax.axis_index("rep")
    n_aux = lax.axis_size("aux")
    n_rep = lax.axis_size("rep")
    full_orbitals = all_rows(orbitals)
    regrouped = lax.all_to_all(density_slab, "aux", split_axis=0, concat_axis=1, tiled=True)
    contracted = jnp.einsum("kpq,qs->kps", regrouped, orbitals, preferred_element_type=jnp.float32)
    partial_w = jnp.sum(full_orbitals[None] * contracted, axis=1)
    summed = lax.psum(partial_w, "rep")
    own_w = lax.all_gather(summed, "aux", axis=0, tiled=True)
    all_w = spread_points(own_w)
    col_width = all_w.shape[1] // (n_aux * n_rep)
    column_w = lax.dynamic_slice_in_dim(
        all_w, (aux_index * n_rep + rep_index) * col_width, col_width, 1
    )
    share = jnp.dot(
        own_w.T, column_w, precision=lax.Precision.HIGHEST, preferred_element_type=jnp.float32
    )
    return share / jnp.float32(own_w.shape[0])


def solution(mesh):
    return jax.shard_map(
        per_device,
        mesh=mesh,
        in_specs=(P("groups", "aux", "rep"), P(("groups", "rep"), "pts")),
        out_specs=P(("groups", "pts"), ("aux", "rep")),
        check_vma=False,
    )
```

profile of v0, /device:TPU:0, one launch (start us, length us, event | category | flops | bytes accessed | tf_op | source)
XLA Modules:
  0.0 205.3 jit_solution(8422975068167474057)
XLA Ops:
  6.5 0.0 all-gather.3.cloned.1.call-start
  6.5 0.7 all-gather.3.cloned.1.call-update
  7.3 0.0 all-reduce.2.cloned.1.call-start
  7.3 99.5 %all_to_all.18 = bf16[16,256,512]{2,1,0:T(8,128)(2,1)S(1)} all-to-all(bf16[16,256,512]{2,1,0:T(8,128)(2,1)} %param.2), channel_id=1, replica_groups=mesh['groups'=2,'aux'=4,'pts'=2,'rep'=2] {'aux'}, dimensions={0} | all-to-all | bytes 8388608 | tf_op jit(solution)/shard_map/all_to_all | solution.py:21
  106.8 2.4 %copy.4 = bf16[4,4,256,512]{3,2,0,1:T(8,128)(2,1)} copy(bf16[4,4,256,512]{3,2,1,0:T(8,128)(2,1)S(1)} %bitcast.10) | data formatting | bytes 8388608 | tf_op jit(solution)/shard_map/all_to_all | solution.py:21
  109.2 0.0 all-gather.3.cloned.1.call-done
  109.2 0.0 copy-start
  109.2 12.0 %convert_element_type.4 = f32[1024,4096]{1,0:T(8,128)} convert(bf16[1024,4096]{1,0:T(8,128)(2,1)} %all-gather.3.cloned.1.call-done) | non-fusion elementwise | flops 4194304 | bytes 25165824 | tf_op jit(solution)/shard_map/convert_element_type | solution.py:23
  121.1 0.0 copy-done
  121.1 22.4 %multiply_reduce_fusion = f32[4,4096]{1,0:T(4,128)} fusion(bf16[4,1024,512]{2,1,0:T(8,128)(2,1)} %bitcast.11, f32[1024,4096]{1,0:T(8,128)} %convert_element_type.4, bf16[512,4096]{1,0:T(8,128)(2,1)S(1)} %copy-done), kind=kOutput, calls=%fused_computation | convolution fusion | flops 17213407232 | bytes 25231360 | tf_op jit(solution)/shard_map/kpq,qs->kps/dot_general | solution.py:22
  143.5 0.0 all-reduce.2.cloned.1.call-update
  143.6 17.2 %all-reduce.2.cloned.1.call-done = f32[4,4096]{1,0:T(4,128)} async-done(((f32[4,4096]{1,0:T(4,128)}), f32[4,4096]{1,0:T(4,128)}) %all-reduce.2.cloned.1.call-update) | async-done | bytes 65552 | tf_op jit(solution)/shard_map/psum | solution.py:24
  160.8 14.4 %all-gather = f32[4,4,4096]{2,1,0:T(4,128)S(1)} all-gather(f32[1,4,4096]{2,1,0:T(4,128)} %bitcast.12), channel_id=1, replica_groups=mesh['groups'=2,'aux'=4,'pts'=2,'rep'=2] {'aux'}, dimensions={0}, use_global_device_ids=true | all-gather | bytes 327680 | tf_op jit(solution)/shard_map/all_gather | solution.py:25
  175.2 0.1 reshape.3
  175.3 7.2 %all_gather.11 = f32[16,8192]{1,0:T(8,128)S(1)} all-gather(f32[16,4096]{1,0:T(8,128)S(1)} %reshape.3), channel_id=1, replica_groups=mesh['groups'=2,'aux'=4,'pts'=2,'rep'=2] {'pts'}, dimensions={1}, use_global_device_ids=true | all-gather | bytes 786432 | tf_op jit(solution)/shard_map/all_gather | solution.py:8
  182.6 15.9 %convolution_multiply_fusion = f32[4096,1024]{1,0:T(8,128)} fusion(f32[16,4096]{1,0:T(8,128)S(1)} %reshape.3, f32[16,8192]{1,0:T(8,128)S(1)} %all_gather.11, s32[]{:T(128)S(6)} %select_n.3), kind=kOutput, calls=%fused_computation.1 | convolution fusion | flops 809500672 | bytes 17104900 | tf_op jit(solution)/shard_map/dot_general | solution.py:31
Async XLA Ops:
  6.5 102.6 %all-gather.3.cloned.1.call-start = ((), (), s32[]{:S(2)}) async-start(), calls=%async_computation.1 | async-start | bytes 12582912 | tf_op jit(solution)/shard_map/all_gather | solution.py:12
  7.3 153.5 %all-reduce.2.cloned.1.call-start = ((), (), s32[]{:S(2)}) async-start(), calls=%async_computation.2 | async-start | bytes 131072 | tf_op jit(solution)/shard_map/psum | solution.py:24
  109.2 12.0 %copy-start = (bf16[512,4096]{1,0:T(8,128)(2,1)S(1)}, bf16[512,4096]{1,0:T(8,128)(2,1)}, u32[]{:S(2)}) copy-start(bf16[512,4096]{1,0:T(8,128)(2,1)} %param.3) | copy-start | bytes 12582916
Sparse Core Ops, SparseCore 0:
  8.9 22.5 all-gather.2
  143.7 17.0 all-reduce.1
where the time goes:
time: 206 us; the launch traced here: 205 us
  blocking collectives  121 us (59%)
  matrix products  38.3 us (19%)
  waiting for transfers between devices  18 us (9%)
  between operations  13.4 us (7%)
  other arithmetic  12 us (6%)
  local copies, waits for them, and re-layouts  2.48 us (1%)
    all_to_all x1, blocking collectives, per_device(): lax.all_to_all(density_slab, 'aux', split_axis=0, concat_axis=1, tiled=True)  99.5 us
    dot_general x1, matrix products, per_device(): jnp.einsum('kpq,qs->kps', regrouped, orbitals, preferred_element_type=jnp...  22.4 us
    psum x1, waiting for transfers between devices, per_device(): summed = lax.psum(partial_w, 'rep')  17.2 us
    dot_general x1, matrix products, per_device(): jnp.dot(own_w.T, column_w, precision=lax.Precision.HIGHEST, preferred_ele...  15.9 us
    all_gather x1, blocking collectives, per_device(): own_w = lax.all_gather(summed, 'aux', axis=0, tiled=True)  14.4 us
    convert_element_type x1, other arithmetic, per_device(): partial_w = jnp.sum(full_orbitals[None] * contracted, axis=1)  12 us
    all_gather x1, blocking collectives, spread_points(): return lax.all_gather(own_weights, 'pts', axis=1, tiled=True)  7.24 us
  transfers between devices with their start and end apart: 2, of which 1 were waited for; matrix products, arithmetic and copies ran while one was open for 1% of the time, Pallas kernels for 0%

commit v1 on v0

v1 whole, which is shorter than its diff:
```python
import functools

import jax
import jax.numpy as jnp
from jax import lax
from jax.experimental import pallas as pl
from jax.experimental.pallas import tpu as pltpu
from jax.sharding import PartitionSpec as P

MIB = 1 << 20
ROWS = 256


def weights_kernel(
    tiles, width, block, depth, info, d_hbm, c_hbm, far_hbm, w_ref,
    d_buf, c_buf, p_buf, d_sem, c_sem, p_sem,
):
    core, near, first_row = info[0], info[1], info[2]
    n_groups, rows, _ = d_buf.shape
    span = rows // depth

    def parts(t):
        made = []
        for own, half, start in tiles[t]:
            quarter = core if own else 1 - core
            made.append(pl.multiple_of((quarter * 2 + half) * block + start, 128))
        return made

    def c_copies(t):
        return [
            pltpu.make_async_copy(
                c_hbm.at[:, pl.ds(at, width)], c_buf.at[t % 2, :, pl.ds(i * width, width)], c_sem.at[t % 2]
            )
            for i, at in enumerate(parts(t))
        ]

    def p_start(t):
        for i, at in enumerate(parts(t)):
            to = p_buf.at[t % 2, :, pl.ds(i * width, width)]

            @pl.when(near == 1)
            def _():
                rows_at = pl.ds(pl.multiple_of(first_row, 16), depth)
                pltpu.make_async_copy(c_hbm.at[rows_at, pl.ds(at, width)], to, p_sem.at[t % 2]).start()

            @pl.when(near != 1)
            def _():
                pltpu.make_async_copy(far_hbm.at[:, pl.ds(at, width)], to, p_sem.at[t % 2]).start()

    def p_wait(t):
        for i, at in enumerate(parts(t)):
            to = p_buf.at[t % 2, :, pl.ds(i * width, width)]
            pltpu.make_async_copy(far_hbm.at[:, pl.ds(at, width)], to, p_sem.at[t % 2]).wait()

    def d_copy(g):
        return pltpu.make_async_copy(d_hbm.at[g], d_buf.at[g], d_sem.at[g])

    for copy in c_copies(0):
        copy.start()
    d_copy(0).start()
    p_start(0)
    for g in range(1, n_groups):
        d_copy(g).start()
    for t in range(len(tiles)):
        if t + 1 < len(tiles):
            for copy in c_copies(t + 1):
                copy.start()
            p_start(t + 1)
        for copy in c_copies(t):
            copy.wait()
        if t == 0:
            d_copy(0).wait()
        p_wait(t)
        points = c_buf[t % 2]
        factor = p_buf[t % 2].astype(jnp.float32)
        for g in range(n_groups):
            if t == 0 and g:
                d_copy(g).wait()
            product = jnp.dot(d_buf[g], points, preferred_element_type=jnp.float32)
            summed = jnp.sum(product.reshape(span, depth, -1) * factor[None], axis=1)
            for i in range(len(tiles[t])):
                w_ref[t, i, g * span : (g + 1) * span, :] = summed[:, i * width : (i + 1) * width]


def partial_weights(info, d_rows, orbitals, far, tiles, width, block, depth, n_k):
    q = orbitals.shape[0]
    n_groups = d_rows.shape[0]
    held = len(tiles[0])
    any_space = pl.BlockSpec(memory_space=pl.ANY)
    return pl.pallas_call(
        functools.partial(weights_kernel, tiles, width, block, depth),
        grid_spec=pltpu.PrefetchScalarGridSpec(
            num_scalar_prefetch=1,
            grid=(),
            in_specs=[any_space, any_space, any_space],
            out_specs=pl.BlockSpec(memory_space=pltpu.VMEM),
            scratch_shapes=[
                pltpu.VMEM(d_rows.shape, jnp.bfloat16),
                pltpu.VMEM((2, q, held * width), jnp.bfloat16),
                pltpu.VMEM((2, depth, held * width), jnp.bfloat16),
                pltpu.SemaphoreType.DMA((n_groups,)),
                pltpu.SemaphoreType.DMA((2,)),
                pltpu.SemaphoreType.DMA((2,)),
            ],
        ),
        out_shape=jax.ShapeDtypeStruct((len(tiles), held, n_k, width), jnp.float32),
        compiler_params=pltpu.CompilerParams(vmem_limit_bytes=48 * MIB),
        cost_estimate=pl.CostEstimate(
            flops=2 * n_groups * d_rows.shape[1] * q * len(tiles) * held * width,
            bytes_accessed=2 * (d_rows.size + len(tiles) * held * width * (q + depth)),
            transcendentals=0,
        ),
        name="weights",
    )(info, d_rows, orbitals, far)


def split(x):
    high = x.astype(jnp.bfloat16)
    rest = x - high.astype(jnp.float32)
    middle = rest.astype(jnp.bfloat16)
    low = (rest - middle.astype(jnp.float32)).astype(jnp.bfloat16)
    return high, middle, low


def outer_kernel(scale, n_rows, info, *refs):
    own, other, columns, out = refs[:n_rows], refs[n_rows : 2 * n_rows], refs[2 * n_rows], refs[-1]
    step = pl.program_id(0)

    high, middle, low = split(columns[...] * scale)
    right = jnp.concatenate([high, middle, high, low, middle, high], axis=0)

    def fill(chunks):
        at = 0
        for chunk in chunks:
            high, middle, low = split(chunk[0])
            left = jnp.concatenate([high, high, middle, high, middle, low], axis=0)
            out[at : at + left.shape[1], :] = lax.dot_general(
                left, right, (((0,), (0,)), ((), ())), preferred_element_type=jnp.float32
            )
            at += left.shape[1]

    @pl.when(step < 2)
    def _():
        fill(own)

    @pl.when(step >= 2)
    def _():
        fill(other)


def outer(info, own, other, columns, out_shape, at, before=None):
    n_k, width = columns.shape
    block = out_shape[0] // 4
    row_specs = [
        pl.BlockSpec((1, n_k, x.shape[2]), lambda i, info: (jnp.minimum(i, 1), 0, 0)) for x in own
    ] + [
        pl.BlockSpec((1, n_k, x.shape[2]), lambda i, info: (jnp.maximum(i - 2, 0), 0, 0)) for x in other
    ]
    args = [*own, *other, columns]
    specs = [*row_specs, pl.BlockSpec((n_k, width), lambda i, info: (0, 0))]
    aliases = {}
    if before is not None:
        aliases = {len(args) + 1: 0}
        args.append(before)
        specs.append(pl.BlockSpec(memory_space=pl.ANY))

    def place(i, info):
        quarter = jnp.where(i < 2, info[0], 1 - info[0])
        return quarter * 2 + i % 2, at // width

    return pl.pallas_call(
        functools.partial(outer_kernel, 1.0 / n_k, len(own)),
        grid_spec=pltpu.PrefetchScalarGridSpec(
            num_scalar_prefetch=1,
            grid=(4,),
            in_specs=specs,
            out_specs=pl.BlockSpec((block, width), place),
        ),
        out_shape=jax.ShapeDtypeStruct(out_shape, jnp.float32),
        input_output_aliases=aliases,
        compiler_params=pltpu.CompilerParams(vmem_limit_bytes=48 * MIB),
        cost_estimate=pl.CostEstimate(
            flops=2 * 6 * n_k * out_shape[0] * width, bytes_accessed=4 * out_shape[0] * width, transcendentals=0
        ),
        name="outer",
    )(info, *args)


def swap(x):
    return lax.ppermute(x, "rep", [(0, 1), (1, 0)])


def sum_aux(x, n_aux):
    total = x
    for shift in range(1, n_aux):
        total = total + lax.ppermute(x, "aux", [(i, i ^ shift) for i in range(n_aux)])
    return total


def per_device(n_aux, n_pts, density_slab, orbitals):
    aux, pts, core = lax.axis_index("aux"), lax.axis_index("pts"), lax.axis_index("rep")
    n_k, depth, q = density_slab.shape
    points = orbitals.shape[1]
    block = points // 4
    late = max(block // 4, 128)
    early = block - late
    d_rows = density_slab.reshape(-1, ROWS, q)

    per_core = n_aux // 2
    near = (aux // per_core == core).astype(jnp.int32)
    first_row = (aux % per_core) * depth
    info = jnp.stack([core.astype(jnp.int32), near, first_row.astype(jnp.int32)])
    far = swap(lax.dynamic_slice_in_dim(orbitals, first_row, depth, 0))

    weigh = functools.partial(partial_weights, info, d_rows, orbitals, far, block=block, depth=depth, n_k=n_k)

    def gather(total):
        other = swap(total)
        held = jnp.where(aux % 2 == core, total, other)
        return other, lax.dynamic_index_in_dim(held, core, 0, keepdims=False)

    home = n_aux // n_pts

    def columns_of(held):
        got = held
        for shift in range(1, n_pts):
            pairs = [(a * n_pts + a // home, a * n_pts + (a // home + shift) % n_pts) for a in range(n_aux)]
            came = lax.ppermute(held, ("aux", "pts"), pairs)
            got = jnp.where((pts - aux // home) % n_pts == shift, came, got)
        return got

    a = weigh(tiles=[[(0, 0, 0)], [(0, 1, 0)], [(1, 0, 0)], [(1, 1, 0)]], width=early)[:, 0]
    a_came = swap(a[:2])
    b_send = weigh(tiles=[[(0, 0, early), (0, 1, early)]], width=late)[0]
    a_total = sum_aux(a[2:] + a_came, n_aux)
    b_came = swap(b_send)
    b_keep = weigh(tiles=[[(1, 0, early), (1, 1, early)]], width=late)[0]
    b_total = sum_aux(b_keep + b_came, n_aux)
    a_other, a_held = gather(a_total)
    a_columns = columns_of(a_held)
    b_other, b_held = gather(b_total)
    b_columns = columns_of(b_held)

    out_shape = (points, block)
    own, other = [a_total, b_total], [a_other, b_other]
    first = outer(info, own, other, a_columns, out_shape, 0)
    return outer(info, own, other, b_columns, out_shape, early, first)


def solution(mesh):
    shape = mesh.shape
    return jax.shard_map(
        functools.partial(per_device, shape["aux"], shape["pts"]),
        mesh=mesh,
        in_specs=(P("groups", "aux", "rep"), P(("groups", "rep"), "pts")),
        out_specs=P(("groups", "pts"), ("aux", "rep")),
        check_vma=False,
    )
```

time: 206 us -> 76.3 us (0.37)
  blocking collectives: 121 us -> 0 us
  Pallas kernels: 0 us -> 43.3 us
  matrix products: 38.3 us -> 0 us
  starting transfers between devices: 0.04 us -> 15.9 us
  between operations: 13.4 us -> 0.14 us
  other arithmetic: 12 us -> 0.17 us
  waiting for transfers between devices: 18 us -> 13.4 us
    all_to_all x1 -> x0, blocking collectives: 99.5 us -> none  [per_device(): lax.all_to_all(density_slab, 'aux', split_axis=0, concat_axis=1, tiled=True)]
    pallas_call x0 -> x5, Pallas kernels: none -> 43.3 us  [the longest x3 33.6 us: partial_weights(): pl.pallas_call(functools.partial(weights_kernel, tiles, width, block, dep...]
    dot_general x2 -> x0, matrix products: 38.3 us -> none  [the longest x1 22.4 us: per_device(): jnp.einsum('kpq,qs->kps', regrouped, orbitals, preferred_element_type=jnp...]
    all_gather x2 -> x0, blocking collectives: 21.7 us -> none  [the longest x1 14.4 us: per_device(): own_w = lax.all_gather(summed, 'aux', axis=0, tiled=True)]
    psum x1 -> x0, waiting for transfers between devices: 17.2 us -> none  [per_device(): summed = lax.psum(partial_w, 'rep')]
    ppermute x0 -> x13, starting transfers between devices: none -> 15.9 us  [the longest x6 10 us: sum_aux(): lax.ppermute(x, 'aux', [(i, i ^ shift) for i in range(n_aux)])]
    ppermute x0 -> x13, waiting for transfers between devices: none -> 13.4 us  [the longest x6 7.72 us: sum_aux(): lax.ppermute(x, 'aux', [(i, i ^ shift) for i in range(n_aux)])]
    convert_element_type x1 -> x0, other arithmetic: 12 us -> none  [per_device(): partial_w = jnp.sum(full_orbitals[None] * contracted, axis=1)]
  transfers between devices with their start and end apart: 2 -> 13, of which waited for: 1 -> 6; matrix products, arithmetic and copies ran while one was open for 1% -> 0% of each run, Pallas kernels for 0% -> 35%
where the time goes in v1:
time: 76.3 us; the launch traced here: 76.1 us
  Pallas kernels  43.3 us (57%)
  starting transfers between devices  15.9 us (21%)
  waiting for transfers between devices  13.4 us (18%)
  local copies, waits for them, and re-layouts  3.14 us (4%)
    pallas_call x3, Pallas kernels, partial_weights(): pl.pallas_call(functools.partial(weights_kernel, tiles, width, block, dep...  33.6 us
    ppermute x6, starting transfers between devices, sum_aux(): lax.ppermute(x, 'aux', [(i, i ^ shift) for i in range(n_aux)])  10 us
    pallas_call x2, Pallas kernels, outer(): pl.pallas_call(functools.partial(outer_kernel, 1.0 / n_k, len(own)), grid...  9.73 us
    ppermute x6, waiting for transfers between devices, sum_aux(): lax.ppermute(x, 'aux', [(i, i ^ shift) for i in range(n_aux)])  7.72 us
    ppermute x2, starting transfers between devices, columns_of(): came = lax.ppermute(held, ('aux', 'pts'), pairs)  4.69 us
    ppermute x5, waiting for transfers between devices, swap(): return lax.ppermute(x, 'rep', [(0, 1), (1, 0)])  3.93 us
    dynamic_slice x1, local copies, waits for them, and re-layouts, per_device(): far = swap(lax.dynamic_slice_in_dim(orbitals, first_row, depth, 0))  3.13 us
    ppermute x2, waiting for transfers between devices, columns_of(): came = lax.ppermute(held, ('aux', 'pts'), pairs)  1.73 us
  transfers between devices with their start and end apart: 13, of which 6 were waited for; matrix products, arithmetic and copies ran while one was open for 0% of the time, Pallas kernels for 35%

profile of v1, /device:TPU:0, one launch (start us, length us, event | category | flops | bytes accessed | tf_op | source)
XLA Modules:
  0.0 76.1 jit_solution(9253865676879175379)
XLA Ops:
  0.0 3.1 %constant_dynamic-slice_fusion = bf16[256,4096]{1,0:T(8,128)(2,1)} fusion(bf16[512,4096]{1,0:T(8,128)(2,1)} %c_hbm.5, s32[]{:T(128)S(6)} %select_n.66), kind=kLoop, calls=%fused_computation.12 | loop fusion | bytes 4194308 | tf_op jit(solution)/shard_map/dynamic_slice | solution.py:213
  3.1 0.5 collective-permute-start
  3.6 0.1 pad_add_fusion.info
  3.7 3.9 %collective-permute-done.far_hbm = bf16[256,4096]{1,0:T(8,128)(2,1)S(1)} collective-permute-done((bf16[256,4096]{1,0:T(8,128)(2,1)}, bf16[256,4096]{1,0:T(8,128)(2,1)S(1)}, u32[]{:S(2)}, u32[]{:S(2)}) %collective-permute-start) | collective-permute-done | bytes 2097184 | tf_op jit(solution)/shard_map/ppermute | solution.py:190
  7.6 6.9 %weights.5 = f32[1,2,16,256]{3,2,1,0:T(8,128)S(1)} custom-call(s32[3]{0:T(128)S(1)} %pad_add_fusion.info, bf16[16,256,512]{2,1,0:T(8,128)(2,1)} %d_hbm.5, bf16[512,4096]{1,0:T(8,128)(2,1)} %c_hbm.5, bf16[256,4096]{1,0:T(8,128)(2,1)S(1)} %collective-permute-done.far_hbm), custom_call_target="tpu_custom_call" | custom-call | flops 2147483648 | bytes 4980736 | tf_op jit(solution)/shard_map/weights/pallas_call | solution.py:90
  14.5 0.4 collective-permute-start.5
  14.9 19.8 %weights.3 = f32[4,1,16,768]{3,2,1,0:T(8,128)S(1)} custom-call(s32[3]{0:T(128)S(1)} %pad_add_fusion.info, bf16[16,256,512]{2,1,0:T(8,128)(2,1)} %d_hbm.5, bf16[512,4096]{1,0:T(8,128)(2,1)} %c_hbm.5, bf16[256,4096]{1,0:T(8,128)(2,1)S(1)} %collective-permute-done.far_hbm), custom_call_target="tpu_custom_call" | custom-call | flops 12884901888 | bytes 8912896 | tf_op jit(solution)/shard_map/weights/pallas_call | solution.py:90
  34.7 0.3 collective-permute-start.1
  34.9 6.9 %weights.4 = f32[1,2,16,256]{3,2,1,0:T(8,128)S(1)} custom-call(s32[3]{0:T(128)S(1)} %pad_add_fusion.info, bf16[16,256,512]{2,1,0:T(8,128)(2,1)} %d_hbm.5, bf16[512,4096]{1,0:T(8,128)(2,1)} %c_hbm.5, bf16[256,4096]{1,0:T(8,128)(2,1)S(1)} %collective-permute-done.far_hbm), custom_call_target="tpu_custom_call" | custom-call | flops 2147483648 | bytes 4980736 | tf_op jit(solution)/shard_map/weights/pallas_call | solution.py:90
  41.9 4.9 %collective-permute-start.8 = (f32[2,16,256]{2,1,0:T(8,128)S(1)}, f32[2,16,256]{2,1,0:T(8,128)S(1)}, u32[]{:S(2)}, u32[]{:S(2)}) collective-permute-start(f32[2,16,256]{2,1,0:T(8,128)S(1)} %bitcast_add_fusion), channel_id=1, source_target_pairs={{0,12},{4,8},{8,4},{12,0},{1,13},{5,9},{9,5},{13,1},{2,14},{6,10},... | collective-permute-start | bytes 98312 | tf_op jit(solution)/shard_map/ppermute | solution.py:196
  46.8 0.6 collective-permute-start.6
  47.5 3.8 %collective-permute-start.4 = (f32[2,16,768]{2,1,0:T(8,128)S(1)}, f32[2,16,768]{2,1,0:T(8,128)S(1)}, u32[]{:S(2)}, u32[]{:S(2)}) collective-permute-start(f32[2,16,768]{2,1,0:T(8,128)S(1)} %fusion), channel_id=1, source_target_pairs={{0,12},{4,8},{8,4},{12,0},{1,13},{5,9},{9,5},{13,1},{2,14},{6,10},... | collective-permute-start | bytes 294920 | tf_op jit(solution)/shard_map/ppermute | solution.py:196
  51.3 0.6 collective-permute-start.2
  51.9 1.1 %collective-permute-done.7 = f32[2,16,256]{2,1,0:T(8,128)S(1)} collective-permute-done((f32[2,16,256]{2,1,0:T(8,128)S(1)}, f32[2,16,256]{2,1,0:T(8,128)S(1)}, u32[]{:S(2)}, u32[]{:S(2)}) %collective-permute-start.7) | collective-permute-done | bytes 32800 | tf_op jit(solution)/shard_map/ppermute | solution.py:196
  53.0 0.1 collective-permute-start.10
  53.1 2.5 %collective-permute-done.4 = f32[2,16,768]{2,1,0:T(8,128)S(1)} collective-permute-done((f32[2,16,768]{2,1,0:T(8,128)S(1)}, f32[2,16,768]{2,1,0:T(8,128)S(1)}, u32[]{:S(2)}, u32[]{:S(2)}) %collective-permute-start.4) | collective-permute-done | bytes 98336 | tf_op jit(solution)/shard_map/ppermute | solution.py:196
  55.6 4.1 %collective-permute-done.3 = f32[2,16,768]{2,1,0:T(8,128)S(1)} collective-permute-done((f32[2,16,768]{2,1,0:T(8,128)S(1)}, f32[2,16,768]{2,1,0:T(8,128)S(1)}, u32[]{:S(2)}, u32[]{:S(2)}) %collective-permute-start.3) | collective-permute-done | bytes 98336 | tf_op jit(solution)/shard_map/ppermute | solution.py:196
  59.8 0.1 collective-permute-start.9
  59.9 3.4 %collective-permute-start.11 = (f32[16,256]{1,0:T(8,128)S(1)}, f32[16,256]{1,0:T(8,128)S(1)}, u32[]{:S(2)}, u32[]{:S(2)}) collective-permute-start(f32[16,256]{1,0:T(8,128)S(1)} %fusion.2), channel_id=1, source_target_pairs={{0,2},{4,6},{10,8},{14,12},{1,3},{5,7},{11,9},{15,13},{16,18},{20,... | collective-permute-start | bytes 49160 | tf_op jit(solution)/shard_map/ppermute | solution.py:228
  63.3 1.3 %collective-permute-start.12 = (f32[16,768]{1,0:T(8,128)S(1)}, f32[16,768]{1,0:T(8,128)S(1)}, u32[]{:S(2)}, u32[]{:S(2)}) collective-permute-start(f32[16,768]{1,0:T(8,128)S(1)} %fusion.1), channel_id=1, source_target_pairs={{0,2},{4,6},{10,8},{14,12},{1,3},{5,7},{11,9},{15,13},{16,18},{20,... | collective-permute-start | bytes 147464 | tf_op jit(solution)/shard_map/ppermute | solution.py:228
  64.6 0.1 collective-permute-done.11
  64.7 1.6 %collective-permute-done.12 = f32[16,768]{1,0:T(8,128)S(1)} collective-permute-done((f32[16,768]{1,0:T(8,128)S(1)}, f32[16,768]{1,0:T(8,128)S(1)}, u32[]{:S(2)}, u32[]{:S(2)}) %collective-permute-start.12) | collective-permute-done | bytes 49184 | tf_op jit(solution)/shard_map/ppermute | solution.py:228
  66.4 6.2 %outer.2.refs_5_ = f32[4096,1024]{1,0:T(8,128)} custom-call(s32[3]{0:T(128)S(1)} %pad_add_fusion.info, f32[2,16,768]{2,1,0:T(8,128)S(1)} %add_add_fusion.refs_0_, f32[2,16,256]{2,1,0:T(8,128)S(1)} %add_add_fusion.1.refs_1_, f32[2,16,768]{2,1,0:T(8,128)S(1)} %collective-permute-done.9.refs_2_, f32[2,16,256]{2,1,0:T(8,128)S(1)} %collective-permute-done.10.refs_3_, ...), custom_call_target="tpu_custom_call" | custom-call | flops 603979776 | bytes 12582912 | tf_op jit(solution)/shard_map/outer/pallas_call | solution.py:171
  72.5 3.6 %outer.3 = f32[4096,1024]{1,0:T(8,128)} custom-call(s32[3]{0:T(128)S(1)} %pad_add_fusion.info, f32[2,16,768]{2,1,0:T(8,128)S(1)} %add_add_fusion.refs_0_, f32[2,16,256]{2,1,0:T(8,128)S(1)} %add_add_fusion.1.refs_1_, f32[2,16,768]{2,1,0:T(8,128)S(1)} %collective-permute-done.9.refs_2_, ...), custom_call_target="tpu_custom_call", output_to_operand_aliasing={{}: (6, {})} | custom-call | flops 201326592 | bytes 4194304 | tf_op jit(solution)/shard_map/outer/pallas_call | solution.py:171
  (18 shorter events, 0.1 us)
Async XLA Ops:
  3.1 4.5 %collective-permute-start = (bf16[256,4096]{1,0:T(8,128)(2,1)}, bf16[256,4096]{1,0:T(8,128)(2,1)S(1)}, u32[]{:S(2)}, u32[]{:S(2)}) collective-permute-start(bf16[256,4096]{1,0:T(8,128)(2,1)} %constant_dynamic-slice_fusion), channel_id=1, source_target_pairs={{0,1},{1,0},{2,3},{3,2},{4,5},{5,4},{6,7},{7,6},{8,9},{9,8},{10,11... | collective-permute-start | bytes 6291464 | tf_op jit(solution)/shard_map/ppermute | solution.py:190
  14.5 27.4 %collective-permute-start.5 = (f32[2,16,256]{2,1,0:T(8,128)S(1)}, f32[2,16,256]{2,1,0:T(8,128)S(1)}, u32[]{:S(2)}, u32[]{:S(2)}) collective-permute-start(f32[2,16,256]{2,1,0:T(8,128)S(1)} %bitcast.19), channel_id=1, source_target_pairs={{0,1},{1,0},{2,3},{3,2},{4,5},{5,4},{6,7},{7,6},{8,9},{9,8},{10,11... | collective-permute-start | bytes 98312 | tf_op jit(solution)/shard_map/ppermute | solution.py:190
  34.7 12.8 %collective-permute-start.1 = (f32[2,16,768]{2,1,0:T(8,128)S(1)}, f32[2,16,768]{2,1,0:T(8,128)S(1)}, u32[]{:S(2)}, u32[]{:S(2)}) collective-permute-start(f32[2,16,768]{2,1,0:T(8,128)S(1)} %slice_bitcast_fusion), channel_id=1, source_target_pairs={{0,1},{1,0},{2,3},{3,2},{4,5},{5,4},{6,7},{7,6},{8,9},{9,8},{10,11... | collective-permute-start | bytes 294920 | tf_op jit(solution)/shard_map/ppermute | solution.py:190
  41.9 9.4 %collective-permute-start.8 = (f32[2,16,256]{2,1,0:T(8,128)S(1)}, f32[2,16,256]{2,1,0:T(8,128)S(1)}, u32[]{:S(2)}, u32[]{:S(2)}) collective-permute-start(f32[2,16,256]{2,1,0:T(8,128)S(1)} %bitcast_add_fusion), channel_id=1, source_target_pairs={{0,12},{4,8},{8,4},{12,0},{1,13},{5,9},{9,5},{13,1},{2,14},{6,10},... | collective-permute-start | bytes 98312 | tf_op jit(solution)/shard_map/ppermute | solution.py:196
  46.8 6.2 %collective-permute-start.7 = (f32[2,16,256]{2,1,0:T(8,128)S(1)}, f32[2,16,256]{2,1,0:T(8,128)S(1)}, u32[]{:S(2)}, u32[]{:S(2)}) collective-permute-start(f32[2,16,256]{2,1,0:T(8,128)S(1)} %bitcast_add_fusion), channel_id=1, source_target_pairs={{0,8},{4,12},{8,0},{12,4},{1,9},{5,13},{9,1},{13,5},{2,10},{6,14},... | collective-permute-start | bytes 98312 | tf_op jit(solution)/shard_map/ppermute | solution.py:196
  46.8 6.2 %collective-permute-start.6 = (f32[2,16,256]{2,1,0:T(8,128)S(1)}, f32[2,16,256]{2,1,0:T(8,128)S(1)}, u32[]{:S(2)}, u32[]{:S(2)}) collective-permute-start(f32[2,16,256]{2,1,0:T(8,128)S(1)} %bitcast_add_fusion), channel_id=1, source_target_pairs={{0,4},{4,0},{8,12},{12,8},{1,5},{5,1},{9,13},{13,9},{2,6},{6,2},{1... | collective-permute-start | bytes 98312 | tf_op jit(solution)/shard_map/ppermute | solution.py:196
  47.5 8.1 %collective-permute-start.4 = (f32[2,16,768]{2,1,0:T(8,128)S(1)}, f32[2,16,768]{2,1,0:T(8,128)S(1)}, u32[]{:S(2)}, u32[]{:S(2)}) collective-permute-start(f32[2,16,768]{2,1,0:T(8,128)S(1)} %fusion), channel_id=1, source_target_pairs={{0,12},{4,8},{8,4},{12,0},{1,13},{5,9},{9,5},{13,1},{2,14},{6,10},... | collective-permute-start | bytes 294920 | tf_op jit(solution)/shard_map/ppermute | solution.py:196
  51.3 8.5 %collective-permute-start.3 = (f32[2,16,768]{2,1,0:T(8,128)S(1)}, f32[2,16,768]{2,1,0:T(8,128)S(1)}, u32[]{:S(2)}, u32[]{:S(2)}) collective-permute-start(f32[2,16,768]{2,1,0:T(8,128)S(1)} %fusion), channel_id=1, source_target_pairs={{0,8},{4,12},{8,0},{12,4},{1,9},{5,13},{9,1},{13,5},{2,10},{6,14},... | collective-permute-start | bytes 294920 | tf_op jit(solution)/shard_map/ppermute | solution.py:196
  51.3 8.5 %collective-permute-start.2 = (f32[2,16,768]{2,1,0:T(8,128)S(1)}, f32[2,16,768]{2,1,0:T(8,128)S(1)}, u32[]{:S(2)}, u32[]{:S(2)}) collective-permute-start(f32[2,16,768]{2,1,0:T(8,128)S(1)} %fusion), channel_id=1, source_target_pairs={{0,4},{4,0},{8,12},{12,8},{1,5},{5,1},{9,13},{13,9},{2,6},{6,2},{1... | collective-permute-start | bytes 294920 | tf_op jit(solution)/shard_map/ppermute | solution.py:196
  53.0 6.8 %collective-permute-start.10 = (f32[2,16,256]{2,1,0:T(8,128)S(1)}, f32[2,16,256]{2,1,0:T(8,128)S(1)}, u32[]{:S(2)}, u32[]{:S(2)}) collective-permute-start(f32[2,16,256]{2,1,0:T(8,128)S(1)} %add_add_fusion.1.refs_1_), channel_id=1, source_target_pairs={{0,1},{1,0},{2,3},{3,2},{4,5},{5,4},{6,7},{7,6},{8,9},{9,8},{10,11... | collective-permute-start | bytes 98312 | tf_op jit(solution)/shard_map/ppermute | solution.py:190
  59.8 3.5 %collective-permute-start.9 = (f32[2,16,768]{2,1,0:T(8,128)S(1)}, f32[2,16,768]{2,1,0:T(8,128)S(1)}, u32[]{:S(2)}, u32[]{:S(2)}) collective-permute-start(f32[2,16,768]{2,1,0:T(8,128)S(1)} %add_add_fusion.refs_0_), channel_id=1, source_target_pairs={{0,1},{1,0},{2,3},{3,2},{4,5},{5,4},{6,7},{7,6},{8,9},{9,8},{10,11... | collective-permute-start | bytes 294920 | tf_op jit(solution)/shard_map/ppermute | solution.py:190
  59.9 4.8 %collective-permute-start.11 = (f32[16,256]{1,0:T(8,128)S(1)}, f32[16,256]{1,0:T(8,128)S(1)}, u32[]{:S(2)}, u32[]{:S(2)}) collective-permute-start(f32[16,256]{1,0:T(8,128)S(1)} %fusion.2), channel_id=1, source_target_pairs={{0,2},{4,6},{10,8},{14,12},{1,3},{5,7},{11,9},{15,13},{16,18},{20,... | collective-permute-start | bytes 49160 | tf_op jit(solution)/shard_map/ppermute | solution.py:228
  63.3 3.0 %collective-permute-start.12 = (f32[16,768]{1,0:T(8,128)S(1)}, f32[16,768]{1,0:T(8,128)S(1)}, u32[]{:S(2)}, u32[]{:S(2)}) collective-permute-start(f32[16,768]{1,0:T(8,128)S(1)} %fusion.1), channel_id=1, source_target_pairs={{0,2},{4,6},{10,8},{14,12},{1,3},{5,7},{11,9},{15,13},{16,18},{20,... | collective-permute-start | bytes 147464 | tf_op jit(solution)/shard_map/ppermute | solution.py:228

commit v2 on v0

v2 whole, which is shorter than its diff:
```python
import functools

import jax
import jax.numpy as jnp
from jax import lax
from jax.experimental import pallas as pl
from jax.experimental.pallas import tpu as pltpu
from jax.sharding import PartitionSpec as P

MIB = 1 << 20
ROWS = 256
SLICE_MIB = 50
HEAD_MIB = 36
WEIGHTS_MIB = 32
MADE = 512
PIECES = 2
OUTER_MIB = 40


def slice_kernel(info, c_hbm, first_ref, second_ref, sem):
    depth, points = first_ref.shape
    rows = pl.ds(pl.multiple_of(info[2], 16), depth)
    copies = []
    for i, (quarter, to) in enumerate(((info[0], first_ref), (1 - info[0], second_ref))):
        there = pl.ds(pl.multiple_of(quarter * points, 128), points)
        copies.append(pltpu.make_async_copy(c_hbm.at[rows, there], to, sem.at[i]))
    for copy in copies:
        copy.start()
    for copy in copies:
        copy.wait()


def head_kernel(width, block, info, d_hbm, c_hbm, d_ref, c_ref, *refs):
    products, (d_sem, c_sem) = refs[:-2], refs[-2:]
    piece = width // len(products)
    n_groups = d_ref.shape[0]
    first = pl.multiple_of((1 - info[0]) * 2 * block, 128)

    def c_copy(at, size, i):
        there = pl.ds(at, size)
        return pltpu.make_async_copy(c_hbm.at[:, there], c_ref.at[:, there], c_sem.at[i])

    stages = [0, 1, 4, n_groups]
    d_copies = [
        pltpu.make_async_copy(d_hbm.at[pl.ds(lo, hi - lo)], d_ref.at[pl.ds(lo, hi - lo)], d_sem.at[i])
        for i, (lo, hi) in enumerate(zip(stages, stages[1:]))
    ]
    near = c_copy(first, width, 0)
    rest = [
        c_copy(first + width, 2 * block - width, 1),
        c_copy(pl.multiple_of(info[0] * 2 * block, 128), 2 * block, 2),
    ]
    near.start()
    for copy in d_copies + rest:
        copy.start()
    near.wait()
    for copy, lo, hi in zip(d_copies, stages, stages[1:]):
        copy.wait()
        for g in range(lo, hi):
            product = jnp.dot(d_ref[g], c_ref[:, pl.ds(first, width)], preferred_element_type=jnp.float32)
            for i, ref in enumerate(products):
                ref[g] = product[:, i * piece : (i + 1) * piece]
    for copy in rest:
        copy.wait()


def weights_kernel(tiles, block, depth, info, d_ref, c_ref, far_ref, *refs):
    made, w_ref = refs[:-1], refs[-1]
    core, near, first_row = info[0], info[1], info[2]
    n_groups, rows, _ = d_ref.shape
    span = rows // depth
    origin = min(tile[2] for tile in tiles)
    for t, (own, half, start, width) in enumerate(tiles):
        at = half * block + start
        there = pl.ds(pl.multiple_of((core if own else 1 - core) * 2 * block + at, 128), width)
        mine = c_ref[pl.ds(pl.multiple_of(first_row, 16), depth), there]
        scale = jnp.where(near == 1, mine, far_ref[:, at : at + width]).astype(jnp.float32)
        ready = t - len(tiles) + len(made)
        for g in range(n_groups):
            if ready >= 0:
                product = made[ready][g]
            else:
                product = jnp.dot(d_ref[g], c_ref[:, there], preferred_element_type=jnp.float32)
            w_ref[half, g * span : (g + 1) * span, start - origin : start - origin + width] = jnp.sum(
                product.reshape(span, depth, width) * scale[None], axis=1
            )


VMEM = pl.BlockSpec(memory_space=pltpu.VMEM)
ANY = pl.BlockSpec(memory_space=pl.ANY)


def own_rows(info, orbitals, depth):
    part = jax.ShapeDtypeStruct((depth, orbitals.shape[1] // 2), jnp.bfloat16)
    return pl.pallas_call(
        slice_kernel,
        grid_spec=pltpu.PrefetchScalarGridSpec(
            num_scalar_prefetch=1, grid=(), in_specs=[ANY], out_specs=[VMEM, VMEM],
            scratch_shapes=[pltpu.SemaphoreType.DMA((2,))],
        ),
        out_shape=[part, part],
        compiler_params=pltpu.CompilerParams(vmem_limit_bytes=SLICE_MIB * MIB),
        name="own_rows",
    )(info, orbitals)


def head(info, d_rows, orbitals, width, block):
    n_groups, rows, q = d_rows.shape
    return pl.pallas_call(
        functools.partial(head_kernel, width, block),
        grid_spec=pltpu.PrefetchScalarGridSpec(
            num_scalar_prefetch=1, grid=(), in_specs=[ANY, ANY], out_specs=[VMEM] * (2 + PIECES),
            scratch_shapes=[pltpu.SemaphoreType.DMA((3,)), pltpu.SemaphoreType.DMA((3,))],
        ),
        out_shape=[
            jax.ShapeDtypeStruct(d_rows.shape, jnp.bfloat16),
            jax.ShapeDtypeStruct(orbitals.shape, jnp.bfloat16),
            *[jax.ShapeDtypeStruct((n_groups, rows, width // PIECES), jnp.float32)] * PIECES,
        ],
        compiler_params=pltpu.CompilerParams(vmem_limit_bytes=HEAD_MIB * MIB),
        cost_estimate=pl.CostEstimate(
            flops=2 * n_groups * rows * q * width, bytes_accessed=2 * (d_rows.size + orbitals.size), transcendentals=0
        ),
        name="head",
    )(info, d_rows, orbitals)


def partial_weights(info, d_rows, orbitals, far, made, tiles, width, block, depth, n_k):
    return pl.pallas_call(
        functools.partial(weights_kernel, tiles, block, depth),
        grid_spec=pltpu.PrefetchScalarGridSpec(
            num_scalar_prefetch=1,
            grid=(),
            in_specs=[VMEM] * (3 + len(made)),
            out_specs=VMEM,
        ),
        out_shape=jax.ShapeDtypeStruct((2, n_k, width), jnp.float32),
        compiler_params=pltpu.CompilerParams(vmem_limit_bytes=WEIGHTS_MIB * MIB),
        cost_estimate=pl.CostEstimate(flops=1, bytes_accessed=0, transcendentals=0),
        name="weights",
    )(info, d_rows, orbitals, far, *made)


def split(x):
    high = x.astype(jnp.bfloat16)
    rest = x - high.astype(jnp.float32)
    middle = rest.astype(jnp.bfloat16)
    low = (rest - middle.astype(jnp.float32)).astype(jnp.bfloat16)
    return high, middle, low


def outer_kernel(scale, at, n_rows, info, *refs):
    own, other, columns = refs[:n_rows], refs[n_rows : 2 * n_rows], refs[2 * n_rows]
    out_hbm, buffer, sems = refs[-3:]
    width = columns.shape[1]
    block = sum(x.shape[2] for x in own)

    high, middle, low = split(columns[...] * scale)
    right = jnp.concatenate([high, middle, high, low, middle, high], axis=0)
    copies = []
    row = 0
    for quarter, chunks in ((info[0], own), (1 - info[0], other)):
        for half in range(2):
            start = 0
            for chunk in chunks:
                size = chunk.shape[2]
                step = min(size, 384 if size % 384 == 0 else 256)
                for lo in range(0, size, step):
                    high, middle, low = split(chunk[half, :, lo : lo + step])
                    left = jnp.concatenate([high, high, middle, high, middle, low], axis=0)
                    buffer[row : row + step, :] = lax.dot_general(
                        left, right, (((0,), (0,)), ((), ())), preferred_element_type=jnp.float32
                    )
                    to = pl.multiple_of((quarter * 2 + half) * block + start + lo, 8)
                    copy = pltpu.make_async_copy(
                        buffer.at[pl.ds(row, step)],
                        out_hbm.at[pl.ds(to, step), pl.ds(at, width)],
                        sems.at[len(copies)],
                    )
                    copy.start()
                    copies.append(copy)
                    row += step
                start += size
    for copy in copies:
        copy.wait()


def outer(info, own, other, columns, out_shape, at, before=None):
    n_k, width = columns.shape
    args = [*own, *other, columns]
    specs = [VMEM] * len(args)
    aliases = {}
    if before is not None:
        aliases = {len(args) + 1: 0}
        args.append(before)
        specs.append(ANY)
    return pl.pallas_call(
        functools.partial(outer_kernel, 1.0 / n_k, at, len(own)),
        grid_spec=pltpu.PrefetchScalarGridSpec(
            num_scalar_prefetch=1,
            grid=(),
            in_specs=specs,
            out_specs=ANY,
            scratch_shapes=[pltpu.VMEM((out_shape[0], width), jnp.float32), pltpu.SemaphoreType.DMA((32,))],
        ),
        out_shape=jax.ShapeDtypeStruct(out_shape, jnp.float32),
        input_output_aliases=aliases,
        compiler_params=pltpu.CompilerParams(vmem_limit_bytes=OUTER_MIB * MIB),
        cost_estimate=pl.CostEstimate(
            flops=2 * 6 * n_k * out_shape[0] * width, bytes_accessed=4 * out_shape[0] * width, transcendentals=0
        ),
        name="outer",
    )(info, *args)


def swap(x):
    return lax.ppermute(x, "rep", [(0, 1), (1, 0)])


def sum_aux(x, n_aux):
    total = x
    for shift in range(1, n_aux):
        total = total + lax.ppermute(x, "aux", [(i, i ^ shift) for i in range(n_aux)])
    return total


def per_device(n_aux, n_pts, density_slab, orbitals):
    aux, pts, core = lax.axis_index("aux"), lax.axis_index("pts"), lax.axis_index("rep")
    n_k, depth, q = density_slab.shape
    points = orbitals.shape[1]
    block = points // 4
    late = max(block // 4, 128)
    early = block - late
    d_rows = density_slab.reshape(-1, ROWS, q)

    per_core = n_aux // 2
    near = (aux // per_core == core).astype(jnp.int32)
    first_row = (aux % per_core) * depth
    info = jnp.stack([core.astype(jnp.int32), near, first_row.astype(jnp.int32)])
    far = [swap(part) for part in own_rows(info, orbitals, depth)]

    ahead = min(early, MADE)
    d_near, c_near, *made = head(info, d_rows, orbitals, ahead, block)

    def weigh(own, width, start, made=(), after=None):
        order = info if after is None else lax.optimization_barrier((info, after))[0]
        tiles = [(own, half, start, width) for half in range(2)]
        if made:
            tiles = [(own, 1, start, width), (own, 0, ahead, width - ahead)]
            tiles += [(own, 0, i * ahead // PIECES, ahead // PIECES) for i in range(PIECES)]
            tiles = [tile for tile in tiles if tile[3]]
        return partial_weights(order, d_near, c_near, far[own], made, tiles, width, block, depth, n_k)

    def gather(total):
        other = swap(total)
        held = jnp.where(aux % 2 == core, total, other)
        return other, lax.dynamic_index_in_dim(held, core, 0, keepdims=False)

    home = n_aux // n_pts

    def columns_of(held):
        got = held
        for shift in range(1, n_pts):
            came = lax.ppermute(held, "pts", [(i, (i + shift) % n_pts) for i in range(n_pts)])
            got = jnp.where((pts - aux // home) % n_pts == shift, came, got)
        return got

    a_send = weigh(0, early, 0, made)
    a_came = swap(a_send)
    a_keep = weigh(1, early, 0, after=a_send)
    a_total = sum_aux(a_keep + a_came, n_aux)
    b_send = weigh(0, late, early, after=a_keep)
    b_came = swap(b_send)
    b_keep = weigh(1, late, early, after=b_send)
    b_partial, a_total = lax.optimization_barrier((b_keep + b_came, a_total))
    a_other, a_held = gather(a_total)
    b_total, a_other, a_columns = lax.optimization_barrier((sum_aux(b_partial, n_aux), a_other, columns_of(a_held)))
    b_other, b_held = gather(b_total)
    b_columns = columns_of(b_held)

    out_shape = (points, block)
    own, other = [a_total, b_total], [a_other, b_other]
    first = outer(info, own, other, a_columns, out_shape, 0)
    return outer(info, own, other, b_columns, out_shape, early, first)


def solution(mesh):
    shape = mesh.shape
    return jax.shard_map(
        functools.partial(per_device, shape["aux"], shape["pts"]),
        mesh=mesh,
        in_specs=(P("groups", "aux", "rep"), P(("groups", "rep"), "pts")),
        out_specs=P(("groups", "pts"), ("aux", "rep")),
        check_vma=False,
    )
```

time: 206 us -> 57.8 us (0.28)
  blocking collectives: 121 us -> 0 us
  matrix products: 38.3 us -> 0 us
  Pallas kernels: 0 us -> 37.1 us
  starting transfers between devices: 0.04 us -> 14.2 us
  between operations: 13.4 us -> 0.35 us
  waiting for transfers between devices: 18 us -> 5.8 us
  other arithmetic: 12 us -> 0.16 us
  local copies, waits for them, and re-layouts: 2.48 us -> 0 us
    all_to_all x1 -> x0, blocking collectives: 99.5 us -> none  [per_device(): lax.all_to_all(density_slab, 'aux', split_axis=0, concat_axis=1, tiled=True)]
    dot_general x2 -> x0, matrix products: 38.3 us -> none  [the longest x1 22.4 us: per_device(): jnp.einsum('kpq,qs->kps', regrouped, orbitals, preferred_element_type=jnp...]
    pallas_call x0 -> x8, Pallas kernels: none -> 37.1 us  [the longest x4 20.9 us: partial_weights(): pl.pallas_call(functools.partial(weights_kernel, tiles, block, depth), gr...]
    all_gather x2 -> x0, blocking collectives: 21.7 us -> none  [the longest x1 14.4 us: per_device(): own_w = lax.all_gather(summed, 'aux', axis=0, tiled=True)]
    psum x1 -> x0, waiting for transfers between devices: 17.2 us -> none  [per_device(): summed = lax.psum(partial_w, 'rep')]
    ppermute x0 -> x14, starting transfers between devices: none -> 14.2 us  [the longest x6 9.85 us: sum_aux(): lax.ppermute(x, 'aux', [(i, i ^ shift) for i in range(n_aux)])]
    convert_element_type x1 -> x0, other arithmetic: 12 us -> none  [per_device(): partial_w = jnp.sum(full_orbitals[None] * contracted, axis=1)]
    ppermute x0 -> x14, waiting for transfers between devices: none -> 5.8 us  [the longest x6 3.35 us: sum_aux(): lax.ppermute(x, 'aux', [(i, i ^ shift) for i in range(n_aux)])]
  transfers between devices with their start and end apart: 2 -> 14, of which waited for: 1 -> 4; matrix products, arithmetic and copies ran while one was open for 1% -> 0% of each run, Pallas kernels for 0% -> 55%
where the time goes in v2:
time: 57.8 us; the launch traced here: 57.6 us
  Pallas kernels  37.1 us (64%)
  starting transfers between devices  14.2 us (25%)
  waiting for transfers between devices  5.8 us (10%)
    pallas_call x4, Pallas kernels, partial_weights(): pl.pallas_call(functools.partial(weights_kernel, tiles, block, depth), gr...  20.9 us
    ppermute x6, starting transfers between devices, sum_aux(): lax.ppermute(x, 'aux', [(i, i ^ shift) for i in range(n_aux)])  9.85 us
    pallas_call x2, Pallas kernels, outer(): pl.pallas_call(functools.partial(outer_kernel, 1.0 / n_k, at, len(own)),...  8.88 us
    pallas_call x1, Pallas kernels, head(): pl.pallas_call(functools.partial(head_kernel, width, block), grid_spec=pl...  5.26 us
    ppermute x6, waiting for transfers between devices, sum_aux(): lax.ppermute(x, 'aux', [(i, i ^ shift) for i in range(n_aux)])  3.35 us
    ppermute x2, starting transfers between devices, columns_of(): lax.ppermute(held, 'pts', [(i, (i + shift) % n_pts) for i in range(n_pts)])  3.05 us
    pallas_call x1, Pallas kernels, own_rows(): pl.pallas_call(slice_kernel, grid_spec=pltpu.PrefetchScalarGridSpec(num_s...  2.1 us
    ppermute x6, starting transfers between devices, swap(): return lax.ppermute(x, 'rep', [(0, 1), (1, 0)])  1.3 us
  transfers between devices with their start and end apart: 14, of which 4 were waited for; matrix products, arithmetic and copies ran while one was open for 0% of the time, Pallas kernels for 55%

profile of v2, /device:TPU:0, one launch (start us, length us, event | category | flops | bytes accessed | tf_op | source)
XLA Modules:
  0.0 57.6 jit_solution(3265231691681496320)
XLA Ops:
  0.0 0.1 pad_add_fusion.info
  0.1 2.1 %own_rows.1 = (bf16[256,2048]{1,0:T(8,128)(2,1)S(1)}, bf16[256,2048]{1,0:T(8,128)(2,1)S(1)}) custom-call(s32[3]{0:T(128)S(1)} %pad_add_fusion.info, bf16[512,4096]{1,0:T(8,128)(2,1)} %c_hbm.3), custom_call_target="tpu_custom_call" | custom-call | tf_op jit(solution)/shard_map/own_rows/pallas_call | solution.py:95
  2.2 0.5 collective-permute-start
  2.7 0.1 collective-permute-start.1
  2.8 5.3 %head.1 = (bf16[16,256,512]{2,1,0:T(8,128)(2,1)S(1)}, bf16[512,4096]{1,0:T(8,128)(2,1)S(1)}, f32[16,256,256]{2,1,0:T(8,128)S(1)}, f32[16,256,256]{2,1,0:T(8,128)S(1)}) custom-call(s32[3]{0:T(128)S(1)} %pad_add_fusion.info, bf16[16,256,512]{2,1,0:T(8,128)(2,1)} %d_hbm.1, bf16[512,4096]{1,0:T(8,128)(2,1)} %c_hbm.3), custom_call_target="tpu_custom_call" | custom-call | flops 2147483648 | bytes 8388608 | tf_op jit(solution)/shard_map/head/pallas_call | solution.py:109
  8.1 6.7 %weights.4 = f32[2,16,768]{2,1,0:T(8,128)S(1)} custom-call(s32[3]{0:T(128)S(1)} %pad_add_fusion.info, bf16[16,256,512]{2,1,0:T(8,128)(2,1)S(1)} %get-tuple-element.19.d_ref, bf16[512,4096]{1,0:T(8,128)(2,1)S(1)} %get-tuple-element.20.c_ref, bf16[256,2048]{1,0:T(8,128)(2,1)S(1)} %collective-permute-done.far_ref, ...), custom_call_target="tpu_custom_call" | custom-call | flops 1 | tf_op jit(solution)/shard_map/weights/pallas_call | solution.py:129
  14.8 0.5 collective-permute-start.3
  15.3 8.1 %weights.5 = f32[2,16,768]{2,1,0:T(8,128)S(1)} custom-call(s32[3]{0:T(128)S(1)} %pad_add_fusion.info, bf16[16,256,512]{2,1,0:T(8,128)(2,1)S(1)} %get-tuple-element.19.d_ref, bf16[512,4096]{1,0:T(8,128)(2,1)S(1)} %get-tuple-element.20.c_ref, bf16[256,2048]{1,0:T(8,128)(2,1)S(1)} %collective-permute-done.1.far_ref), custom_call_target="tpu_custom_call" | custom-call | flops 1 | tf_op jit(solution)/shard_map/weights/pallas_call | solution.py:129
  23.4 4.8 %collective-permute-start.6 = (f32[2,16,768]{2,1,0:T(8,128)S(1)}, f32[2,16,768]{2,1,0:T(8,128)S(1)}, u32[]{:S(2)}, u32[]{:S(2)}) collective-permute-start(f32[2,16,768]{2,1,0:T(8,128)S(1)} %add.43), channel_id=1, source_target_pairs={{0,12},{4,8},{8,4},{12,0},{1,13},{5,9},{9,5},{13,1},{2,14},{6,10},... | collective-permute-start | bytes 294920 | tf_op jit(solution)/shard_map/ppermute | solution.py:223
  28.1 0.6 %collective-permute-start.4 = (f32[2,16,768]{2,1,0:T(8,128)S(1)}, f32[2,16,768]{2,1,0:T(8,128)S(1)}, u32[]{:S(2)}, u32[]{:S(2)}) collective-permute-start(f32[2,16,768]{2,1,0:T(8,128)S(1)} %add.43), channel_id=1, source_target_pairs={{0,4},{4,0},{8,12},{12,8},{1,5},{5,1},{9,13},{13,9},{2,6},{6,2},{1... | collective-permute-start | bytes 294920 | tf_op jit(solution)/shard_map/ppermute | solution.py:223
  28.8 3.0 %weights.6 = f32[2,16,256]{2,1,0:T(8,128)S(1)} custom-call(s32[3]{0:T(128)S(1)} %pad_add_fusion.info, bf16[16,256,512]{2,1,0:T(8,128)(2,1)S(1)} %get-tuple-element.19.d_ref, bf16[512,4096]{1,0:T(8,128)(2,1)S(1)} %get-tuple-element.20.c_ref, bf16[256,2048]{1,0:T(8,128)(2,1)S(1)} %collective-permute-done.far_ref), custom_call_target="tpu_custom_call" | custom-call | flops 1 | tf_op jit(solution)/shard_map/weights/pallas_call | solution.py:129
  31.8 0.1 collective-permute-start.2
  31.9 3.0 %weights.7 = f32[2,16,256]{2,1,0:T(8,128)S(1)} custom-call(s32[3]{0:T(128)S(1)} %pad_add_fusion.info, bf16[16,256,512]{2,1,0:T(8,128)(2,1)S(1)} %get-tuple-element.19.d_ref, bf16[512,4096]{1,0:T(8,128)(2,1)S(1)} %get-tuple-element.20.c_ref, bf16[256,2048]{1,0:T(8,128)(2,1)S(1)} %collective-permute-done.1.far_ref), custom_call_target="tpu_custom_call" | custom-call | flops 1 | tf_op jit(solution)/shard_map/weights/pallas_call | solution.py:129
  35.0 2.0 %collective-permute-done.5 = f32[2,16,768]{2,1,0:T(8,128)S(1)} collective-permute-done((f32[2,16,768]{2,1,0:T(8,128)S(1)}, f32[2,16,768]{2,1,0:T(8,128)S(1)}, u32[]{:S(2)}, u32[]{:S(2)}) %collective-permute-start.5) | collective-permute-done | bytes 98336 | tf_op jit(solution)/shard_map/ppermute | solution.py:223
  37.0 0.1 collective-permute-start.10
  37.1 2.5 %collective-permute-start.9 = (f32[2,16,256]{2,1,0:T(8,128)S(1)}, f32[2,16,256]{2,1,0:T(8,128)S(1)}, u32[]{:S(2)}, u32[]{:S(2)}) collective-permute-start(f32[2,16,256]{2,1,0:T(8,128)S(1)} %add.42), channel_id=1, source_target_pairs={{0,12},{4,8},{8,4},{12,0},{1,13},{5,9},{9,5},{13,1},{2,14},{6,10},... | collective-permute-start | bytes 98312 | tf_op jit(solution)/shard_map/ppermute | solution.py:223
  39.7 1.9 %collective-permute-start.7 = (f32[2,16,256]{2,1,0:T(8,128)S(1)}, f32[2,16,256]{2,1,0:T(8,128)S(1)}, u32[]{:S(2)}, u32[]{:S(2)}) collective-permute-start(f32[2,16,256]{2,1,0:T(8,128)S(1)} %add.42), channel_id=1, source_target_pairs={{0,4},{4,0},{8,12},{12,8},{1,5},{5,1},{9,13},{13,9},{2,6},{6,2},{1... | collective-permute-start | bytes 98312 | tf_op jit(solution)/shard_map/ppermute | solution.py:223
  41.6 1.6 %collective-permute-start.11 = (f32[16,768]{1,0:T(8,128)S(1)}, f32[16,768]{1,0:T(8,128)S(1)}, u32[]{:S(2)}, u32[]{:S(2)}) collective-permute-start(f32[16,768]{1,0:T(8,128)S(1)} %fusion), channel_id=1, source_target_pairs={{0,2},{2,0},{1,3},{3,1},{4,6},{6,4},{5,7},{7,5},{8,10},{10,8},{9,1... | collective-permute-start | bytes 147464 | tf_op jit(solution)/shard_map/ppermute | solution.py:264
  43.2 1.3 %collective-permute-done.8 = f32[2,16,256]{2,1,0:T(8,128)S(1)} collective-permute-done((f32[2,16,256]{2,1,0:T(8,128)S(1)}, f32[2,16,256]{2,1,0:T(8,128)S(1)}, u32[]{:S(2)}, u32[]{:S(2)}) %collective-permute-start.8) | collective-permute-done | bytes 32800 | tf_op jit(solution)/shard_map/ppermute | solution.py:223
  44.5 1.2 %collective-permute-done.11 = f32[16,768]{1,0:T(8,128)S(1)} collective-permute-done((f32[16,768]{1,0:T(8,128)S(1)}, f32[16,768]{1,0:T(8,128)S(1)}, u32[]{:S(2)}, u32[]{:S(2)}) %collective-permute-start.11) | collective-permute-done | bytes 49184 | tf_op jit(solution)/shard_map/ppermute | solution.py:264
  45.8 1.2 %collective-permute-done.12.refs_3_ = f32[2,16,256]{2,1,0:T(8,128)S(1)} collective-permute-done((f32[2,16,256]{2,1,0:T(8,128)S(1)}, f32[2,16,256]{2,1,0:T(8,128)S(1)}, u32[]{:S(2)}, u32[]{:S(2)}) %collective-permute-start.12) | collective-permute-done | bytes 32800 | tf_op jit(solution)/shard_map/ppermute | solution.py:217
  47.0 1.5 %collective-permute-start.13 = (f32[16,256]{1,0:T(8,128)S(1)}, f32[16,256]{1,0:T(8,128)S(1)}, u32[]{:S(2)}, u32[]{:S(2)}) collective-permute-start(f32[16,256]{1,0:T(8,128)S(1)} %fusion.1), channel_id=1, source_target_pairs={{0,2},{2,0},{1,3},{3,1},{4,6},{6,4},{5,7},{7,5},{8,10},{10,8},{9,1... | collective-permute-start | bytes 49160 | tf_op jit(solution)/shard_map/ppermute | solution.py:264
  48.5 5.8 %outer.2.refs_5_ = f32[4096,1024]{1,0:T(8,128)} custom-call(s32[3]{0:T(128)S(1)} %pad_add_fusion.info, f32[2,16,768]{2,1,0:T(8,128)S(1)} %add_add_fusion.refs_0_, f32[2,16,256]{2,1,0:T(8,128)S(1)} %add_add_fusion.1.refs_1_, f32[2,16,768]{2,1,0:T(8,128)S(1)} %collective-permute-done.10.refs_2_, f32[2,16,256]{2,1,0:T(8,128)S(1)} %collective-permute-done.12.refs_3_, ...), custom_call_target="tpu_custom_call" | custom-call | flops 603979776 | bytes 12582912 | tf_op jit(solution)/shard_map/outer/pallas_call | solution.py:197
  54.3 3.1 %outer.3 = f32[4096,1024]{1,0:T(8,128)} custom-call(s32[3]{0:T(128)S(1)} %pad_add_fusion.info, f32[2,16,768]{2,1,0:T(8,128)S(1)} %add_add_fusion.refs_0_, f32[2,16,256]{2,1,0:T(8,128)S(1)} %add_add_fusion.1.refs_1_, f32[2,16,768]{2,1,0:T(8,128)S(1)} %collective-permute-done.10.refs_2_, ...), custom_call_target="tpu_custom_call", output_to_operand_aliasing={{}: (6, {})} | custom-call | flops 201326592 | bytes 4194304 | tf_op jit(solution)/shard_map/outer/pallas_call | solution.py:197
  (21 shorter events, 0.2 us)
Async XLA Ops:
  2.2 5.9 %collective-permute-start = (bf16[256,2048]{1,0:T(8,128)(2,1)S(1)}, bf16[256,2048]{1,0:T(8,128)(2,1)S(1)}, u32[]{:S(2)}, u32[]{:S(2)}) collective-permute-start(bf16[256,2048]{1,0:T(8,128)(2,1)S(1)} %get-tuple-element.21), channel_id=1, source_target_pairs={{0,1},{1,0},{2,3},{3,2},{4,5},{5,4},{6,7},{7,6},{8,9},{9,8},{10,11... | collective-permute-start | bytes 3145736 | tf_op jit(solution)/shard_map/ppermute | solution.py:217
  2.7 12.6 %collective-permute-start.1 = (bf16[256,2048]{1,0:T(8,128)(2,1)S(1)}, bf16[256,2048]{1,0:T(8,128)(2,1)S(1)}, u32[]{:S(2)}, u32[]{:S(2)}) collective-permute-start(bf16[256,2048]{1,0:T(8,128)(2,1)S(1)} %get-tuple-element.25), channel_id=1, source_target_pairs={{0,1},{1,0},{2,3},{3,2},{4,5},{5,4},{6,7},{7,6},{8,9},{9,8},{10,11... | collective-permute-start | bytes 3145736 | tf_op jit(solution)/shard_map/ppermute | solution.py:217
  14.8 8.6 %collective-permute-start.3 = (f32[2,16,768]{2,1,0:T(8,128)S(1)}, f32[2,16,768]{2,1,0:T(8,128)S(1)}, u32[]{:S(2)}, u32[]{:S(2)}) collective-permute-start(f32[2,16,768]{2,1,0:T(8,128)S(1)} %weights.4), channel_id=1, source_target_pairs={{0,1},{1,0},{2,3},{3,2},{4,5},{5,4},{6,7},{7,6},{8,9},{9,8},{10,11... | collective-permute-start | bytes 294920 | tf_op jit(solution)/shard_map/ppermute | solution.py:217
  23.4 11.6 %collective-permute-start.6 = (f32[2,16,768]{2,1,0:T(8,128)S(1)}, f32[2,16,768]{2,1,0:T(8,128)S(1)}, u32[]{:S(2)}, u32[]{:S(2)}) collective-permute-start(f32[2,16,768]{2,1,0:T(8,128)S(1)} %add.43), channel_id=1, source_target_pairs={{0,12},{4,8},{8,4},{12,0},{1,13},{5,9},{9,5},{13,1},{2,14},{6,10},... | collective-permute-start | bytes 294920 | tf_op jit(solution)/shard_map/ppermute | solution.py:223
  28.1 8.9 %collective-permute-start.5 = (f32[2,16,768]{2,1,0:T(8,128)S(1)}, f32[2,16,768]{2,1,0:T(8,128)S(1)}, u32[]{:S(2)}, u32[]{:S(2)}) collective-permute-start(f32[2,16,768]{2,1,0:T(8,128)S(1)} %add.43), channel_id=1, source_target_pairs={{0,8},{4,12},{8,0},{12,4},{1,9},{5,13},{9,1},{13,5},{2,10},{6,14},... | collective-permute-start | bytes 294920 | tf_op jit(solution)/shard_map/ppermute | solution.py:223
  28.1 8.9 %collective-permute-start.4 = (f32[2,16,768]{2,1,0:T(8,128)S(1)}, f32[2,16,768]{2,1,0:T(8,128)S(1)}, u32[]{:S(2)}, u32[]{:S(2)}) collective-permute-start(f32[2,16,768]{2,1,0:T(8,128)S(1)} %add.43), channel_id=1, source_target_pairs={{0,4},{4,0},{8,12},{12,8},{1,5},{5,1},{9,13},{13,9},{2,6},{6,2},{1... | collective-permute-start | bytes 294920 | tf_op jit(solution)/shard_map/ppermute | solution.py:223
  31.8 3.1 %collective-permute-start.2 = (f32[2,16,256]{2,1,0:T(8,128)S(1)}, f32[2,16,256]{2,1,0:T(8,128)S(1)}, u32[]{:S(2)}, u32[]{:S(2)}) collective-permute-start(f32[2,16,256]{2,1,0:T(8,128)S(1)} %weights.6), channel_id=1, source_target_pairs={{0,1},{1,0},{2,3},{3,2},{4,5},{5,4},{6,7},{7,6},{8,9},{9,8},{10,11... | collective-permute-start | bytes 98312 | tf_op jit(solution)/shard_map/ppermute | solution.py:217
  37.0 4.6 %collective-permute-start.10 = (f32[2,16,768]{2,1,0:T(8,128)S(1)}, f32[2,16,768]{2,1,0:T(8,128)S(1)}, u32[]{:S(2)}, u32[]{:S(2)}) collective-permute-start(f32[2,16,768]{2,1,0:T(8,128)S(1)} %add_add_fusion.refs_0_), channel_id=1, source_target_pairs={{0,1},{1,0},{2,3},{3,2},{4,5},{5,4},{6,7},{7,6},{8,9},{9,8},{10,11... | collective-permute-start | bytes 294920 | tf_op jit(solution)/shard_map/ppermute | solution.py:217
  37.1 6.0 %collective-permute-start.9 = (f32[2,16,256]{2,1,0:T(8,128)S(1)}, f32[2,16,256]{2,1,0:T(8,128)S(1)}, u32[]{:S(2)}, u32[]{:S(2)}) collective-permute-start(f32[2,16,256]{2,1,0:T(8,128)S(1)} %add.42), channel_id=1, source_target_pairs={{0,12},{4,8},{8,4},{12,0},{1,13},{5,9},{9,5},{13,1},{2,14},{6,10},... | collective-permute-start | bytes 98312 | tf_op jit(solution)/shard_map/ppermute | solution.py:223
  39.7 4.8 %collective-permute-start.8 = (f32[2,16,256]{2,1,0:T(8,128)S(1)}, f32[2,16,256]{2,1,0:T(8,128)S(1)}, u32[]{:S(2)}, u32[]{:S(2)}) collective-permute-start(f32[2,16,256]{2,1,0:T(8,128)S(1)} %add.42), channel_id=1, source_target_pairs={{0,8},{4,12},{8,0},{12,4},{1,9},{5,13},{9,1},{13,5},{2,10},{6,14},... | collective-permute-start | bytes 98312 | tf_op jit(solution)/shard_map/ppermute | solution.py:223
  39.7 4.8 %collective-permute-start.7 = (f32[2,16,256]{2,1,0:T(8,128)S(1)}, f32[2,16,256]{2,1,0:T(8,128)S(1)}, u32[]{:S(2)}, u32[]{:S(2)}) collective-permute-start(f32[2,16,256]{2,1,0:T(8,128)S(1)} %add.42), channel_id=1, source_target_pairs={{0,4},{4,0},{8,12},{12,8},{1,5},{5,1},{9,13},{13,9},{2,6},{6,2},{1... | collective-permute-start | bytes 98312 | tf_op jit(solution)/shard_map/ppermute | solution.py:223
  41.6 4.2 %collective-permute-start.11 = (f32[16,768]{1,0:T(8,128)S(1)}, f32[16,768]{1,0:T(8,128)S(1)}, u32[]{:S(2)}, u32[]{:S(2)}) collective-permute-start(f32[16,768]{1,0:T(8,128)S(1)} %fusion), channel_id=1, source_target_pairs={{0,2},{2,0},{1,3},{3,1},{4,6},{6,4},{5,7},{7,5},{8,10},{10,8},{9,1... | collective-permute-start | bytes 147464 | tf_op jit(solution)/shard_map/ppermute | solution.py:264
  45.8 1.3 %collective-permute-start.12 = (f32[2,16,256]{2,1,0:T(8,128)S(1)}, f32[2,16,256]{2,1,0:T(8,128)S(1)}, u32[]{:S(2)}, u32[]{:S(2)}) collective-permute-start(f32[2,16,256]{2,1,0:T(8,128)S(1)} %add_add_fusion.1.refs_1_), channel_id=1, source_target_pairs={{0,1},{1,0},{2,3},{3,2},{4,5},{5,4},{6,7},{7,6},{8,9},{9,8},{10,11... | collective-permute-start | bytes 98312 | tf_op jit(solution)/shard_map/ppermute | solution.py:217
  47.0 7.3 %collective-permute-start.13 = (f32[16,256]{1,0:T(8,128)S(1)}, f32[16,256]{1,0:T(8,128)S(1)}, u32[]{:S(2)}, u32[]{:S(2)}) collective-permute-start(f32[16,256]{1,0:T(8,128)S(1)} %fusion.1), channel_id=1, source_target_pairs={{0,2},{2,0},{1,3},{3,1},{4,6},{6,4},{5,7},{7,5},{8,10},{10,8},{9,1... | collective-permute-start | bytes 49160 | tf_op jit(solution)/shard_map/ppermute | solution.py:264

commit v3 on v0

v3 whole, which is shorter than its diff:
```python
import functools

import jax
import jax.numpy as jnp
from jax import lax
from jax.experimental import pallas as pl
from jax.experimental.pallas import tpu as pltpu
from jax.sharding import PartitionSpec as P

MIB = 1 << 20
ROWS = 256
SLICE_MIB = 50
LOAD_MIB = 44
WEIGHTS_MIB = 36
OUTER_MIB = 40
TILE = 512


def first_kernel(c_hbm, rows_ref, sem):
    depth, points = rows_ref.shape
    place = Place(depth, points)
    copy = pltpu.make_async_copy(c_hbm.at[place.rows, place.quarter(1)], rows_ref, sem)
    copy.start()
    copy.wait()


def load_kernel(c_hbm, sent, c_ref, next_ref, rows_ref, sems):
    depth, points = rows_ref.shape
    place = Place(depth, points)
    copies = [
        pltpu.make_async_copy(c_hbm.at[place.rows, place.quarter(0)], rows_ref, sems.at[0]),
        pltpu.make_async_copy(c_hbm.at[:, place.quarter(0)], c_ref, sems.at[1]),
        pltpu.make_async_copy(c_hbm.at[:, place.quarter(1)], next_ref, sems.at[2]),
    ]
    for copy in copies:
        copy.start()
    for copy in copies:
        copy.wait()


class Place:
    def __init__(self, depth, points):
        self.core = lax.axis_index("rep")
        aux = lax.axis_index("aux")
        per_core = lax.axis_size("aux") // 2
        self.near = aux // per_core == self.core
        self.rows = pl.ds(pl.multiple_of(aux % per_core * depth, 16), depth)
        self.points = points

    def quarter(self, own):
        return pl.ds(pl.multiple_of((self.core if own else 1 - self.core) * self.points, 128), self.points)


def weights_kernel(own, chunks, tile, depth, d_ref, c_ref, far_ref, *refs):
    n_groups, rows, _ = d_ref.shape
    span = rows // depth
    points = c_ref.shape[1]
    block = points // 2
    place = Place(depth, points)
    outs = refs
    for (start, width), w_ref in zip(chunks, outs):
        for half in range(2):
            for lo in range(0, width, tile):
                size = min(tile, width - lo)
                there = slice(half * block + start + lo, half * block + start + lo + size)
                scale = jnp.where(place.near, c_ref[place.rows, there], far_ref[:, there]).astype(jnp.float32)
                for g in range(n_groups):
                    product = jnp.dot(d_ref[g], c_ref[:, there], preferred_element_type=jnp.float32)
                    w_ref[half, g * span : (g + 1) * span, lo : lo + size] = jnp.sum(
                        product.reshape(span, depth, size) * scale[None], axis=1
                    )


VMEM = pl.BlockSpec(memory_space=pltpu.VMEM)
ANY = pl.BlockSpec(memory_space=pl.ANY)


def limit(mib):
    return pltpu.CompilerParams(vmem_limit_bytes=mib * MIB)


def first_rows(orbitals, depth):
    return pl.pallas_call(
        first_kernel,
        in_specs=[ANY],
        out_specs=VMEM,
        scratch_shapes=[pltpu.SemaphoreType.DMA],
        out_shape=jax.ShapeDtypeStruct((depth, orbitals.shape[1] // 2), jnp.bfloat16),
        compiler_params=limit(SLICE_MIB),
        name="first_rows",
    )(orbitals)


def load(orbitals, sent, depth):
    q, points = orbitals.shape
    part = jax.ShapeDtypeStruct((q, points // 2), jnp.bfloat16)
    return pl.pallas_call(
        load_kernel,
        in_specs=[ANY, ANY],
        out_specs=[VMEM] * 3,
        scratch_shapes=[pltpu.SemaphoreType.DMA((3,))],
        out_shape=[part, part, jax.ShapeDtypeStruct((depth, points // 2), jnp.bfloat16)],
        compiler_params=limit(LOAD_MIB),
        cost_estimate=pl.CostEstimate(flops=0, bytes_accessed=2 * orbitals.size, transcendentals=0),
        name="load",
    )(orbitals, sent)


def quarter_weights(own, chunks, depth, n_k, d_rows, c_part, far, *more):
    outs = [jax.ShapeDtypeStruct((2, n_k, width), jnp.float32) for _, width in chunks]
    return pl.pallas_call(
        functools.partial(weights_kernel, own, chunks, TILE, depth),
        in_specs=[VMEM] * 3 + [ANY] * len(more),
        out_specs=[VMEM] * len(outs),
        scratch_shapes=[],
        out_shape=outs,
        compiler_params=limit(WEIGHTS_MIB),
        cost_estimate=pl.CostEstimate(
            flops=2 * d_rows.size * c_part.shape[1], bytes_accessed=0, transcendentals=0
        ),
        name="weights",
    )(d_rows, c_part, far, *more)


def split(x):
    high = x.astype(jnp.bfloat16)
    rest = x - high.astype(jnp.float32)
    middle = rest.astype(jnp.bfloat16)
    low = (rest - middle.astype(jnp.float32)).astype(jnp.bfloat16)
    return high, middle, low


def outer_kernel(scale, at, n_rows, *refs):
    own, other, columns = refs[:n_rows], refs[n_rows : 2 * n_rows], refs[2 * n_rows]
    out_hbm, buffer, sems = refs[-3:]
    width = columns.shape[1]
    block = sum(x.shape[2] for x in own)

    high, middle, low = split(columns[...] * scale)
    right = jnp.concatenate([high, middle, high, low, middle, high], axis=0)
    copies = []
    row = 0
    core = lax.axis_index("rep")
    for quarter, chunks in ((core, own), (1 - core, other)):
        for half in range(2):
            start = 0
            for chunk in chunks:
                size = chunk.shape[2]
                step = min(size, 384 if size % 384 == 0 else 256)
                for lo in range(0, size, step):
                    high, middle, low = split(chunk[half, :, lo : lo + step])
                    left = jnp.concatenate([high, high, middle, high, middle, low], axis=0)
                    buffer[row : row + step, :] = lax.dot_general(
                        left, right, (((0,), (0,)), ((), ())), preferred_element_type=jnp.float32
                    )
                    to = pl.multiple_of((quarter * 2 + half) * block + start + lo, 8)
                    copy = pltpu.make_async_copy(
                        buffer.at[pl.ds(row, step)],
                        out_hbm.at[pl.ds(to, step), pl.ds(at, width)],
                        sems.at[len(copies)],
                    )
                    copy.start()
                    copies.append(copy)
                    row += step
                start += size
    for copy in copies:
        copy.wait()


def outer(own, other, columns, out_shape, at, before=None):
    n_k, width = columns.shape
    args = [*own, *other, columns]
    specs = [VMEM] * len(args)
    aliases = {}
    if before is not None:
        aliases = {len(args): 0}
        args.append(before)
        specs.append(ANY)
    return pl.pallas_call(
        functools.partial(outer_kernel, 1.0 / n_k, at, len(own)),
        in_specs=specs,
        out_specs=ANY,
        scratch_shapes=[pltpu.VMEM((out_shape[0], width), jnp.float32), pltpu.SemaphoreType.DMA((32,))],
        out_shape=jax.ShapeDtypeStruct(out_shape, jnp.float32),
        input_output_aliases=aliases,
        compiler_params=limit(OUTER_MIB),
        cost_estimate=pl.CostEstimate(
            flops=2 * 6 * n_k * out_shape[0] * width, bytes_accessed=4 * out_shape[0] * width, transcendentals=0
        ),
        name="outer",
    )(*args)


def swap(x):
    return lax.ppermute(x, "rep", [(0, 1), (1, 0)])


def sum_aux(x, n_aux):
    total = x
    for shift in range(n_aux - 1, 0, -1):
        total = total + lax.ppermute(x, "aux", [(i, i ^ shift) for i in range(n_aux)])
    return total


def per_device(n_aux, n_pts, density_slab, orbitals):
    aux, pts, core = lax.axis_index("aux"), lax.axis_index("pts"), lax.axis_index("rep")
    n_k, depth, q = density_slab.shape
    points = orbitals.shape[1]
    block = points // 4
    chunks = [(0, block)]
    d_rows = density_slab.reshape(-1, ROWS, q)

    sent = first_rows(orbitals, depth)
    far_first = swap(sent)
    c_first, c_second, sent = load(orbitals, sent, depth)
    far_second = swap(sent)
    sends = quarter_weights(False, chunks, depth, n_k, d_rows, c_first, far_first)
    came = [swap(x) for x in sends]
    keeps = quarter_weights(True, chunks, depth, n_k, d_rows, c_second, far_second)
    total = sum_aux(keeps[0] + came[0], n_aux)

    def gather(total):
        other = swap(total)
        held = jnp.where(aux % 2 == core, total, other)
        return other, lax.dynamic_index_in_dim(held, core, 0, keepdims=False)

    home = n_aux // n_pts

    def columns_of(held):
        got = held
        for shift in range(1, n_pts):
            came = lax.ppermute(held, "pts", [(i, (i + shift) % n_pts) for i in range(n_pts)])
            got = jnp.where((pts - aux // home) % n_pts == shift, came, got)
        return got

    other, held = gather(total)
    return outer([total], [other], columns_of(held), (points, block), 0)


def solution(mesh):
    shape = mesh.shape
    return jax.shard_map(
        functools.partial(per_device, shape["aux"], shape["pts"]),
        mesh=mesh,
        in_specs=(P("groups", "aux", "rep"), P(("groups", "rep"), "pts")),
        out_specs=P(("groups", "pts"), ("aux", "rep")),
        check_vma=False,
    )
```

time: 206 us -> 51.4 us (0.25)
  blocking collectives: 121 us -> 0 us
  matrix products: 38.3 us -> 0 us
  Pallas kernels: 0 us -> 28.4 us
  between operations: 13.4 us -> 0.25 us
  other arithmetic: 12 us -> 0.07 us
  starting transfers between devices: 0.04 us -> 8.18 us
  waiting for transfers between devices: 18 us -> 14.3 us
  local copies, waits for them, and re-layouts: 2.48 us -> 0.01 us
    all_to_all x1 -> x0, blocking collectives: 99.5 us -> none  [per_device(): lax.all_to_all(density_slab, 'aux', split_axis=0, concat_axis=1, tiled=True)]
    dot_general x2 -> x0, matrix products: 38.3 us -> none  [the longest x1 22.4 us: per_device(): jnp.einsum('kpq,qs->kps', regrouped, orbitals, preferred_element_type=jnp...]
    pallas_call x0 -> x5, Pallas kernels: none -> 28.4 us  [the longest x2 18 us: quarter_weights(): pl.pallas_call(functools.partial(weights_kernel, own, chunks, TILE, depth...]
    all_gather x2 -> x0, blocking collectives: 21.7 us -> none  [the longest x1 14.4 us: per_device(): own_w = lax.all_gather(summed, 'aux', axis=0, tiled=True)]
    psum x1 -> x0, waiting for transfers between devices: 17.2 us -> none  [per_device(): summed = lax.psum(partial_w, 'rep')]
    ppermute x0 -> x8, waiting for transfers between devices: none -> 14.3 us  [the longest x3 10.3 us: sum_aux(): lax.ppermute(x, 'aux', [(i, i ^ shift) for i in range(n_aux)])]
    convert_element_type x1 -> x0, other arithmetic: 12 us -> none  [per_device(): partial_w = jnp.sum(full_orbitals[None] * contracted, axis=1)]
    ppermute x0 -> x8, starting transfers between devices: none -> 8.18 us  [the longest x3 5.33 us: sum_aux(): lax.ppermute(x, 'aux', [(i, i ^ shift) for i in range(n_aux)])]
  transfers between devices with their start and end apart: 2 -> 8, of which waited for: 1 -> 4; matrix products, arithmetic and copies ran while one was open for 1% -> 0% of each run, Pallas kernels for 0% -> 40%
where the time goes in v3:
time: 51.4 us; the launch traced here: 51.3 us
  Pallas kernels  28.4 us (55%)
  waiting for transfers between devices  14.3 us (28%)
  starting transfers between devices  8.18 us (16%)
    pallas_call x2, Pallas kernels, quarter_weights(): pl.pallas_call(functools.partial(weights_kernel, own, chunks, TILE, depth...  18 us
    ppermute x3, waiting for transfers between devices, sum_aux(): lax.ppermute(x, 'aux', [(i, i ^ shift) for i in range(n_aux)])  10.3 us
    pallas_call x1, Pallas kernels, outer(): pl.pallas_call(functools.partial(outer_kernel, 1.0 / n_k, at, len(own)),...  6.43 us
    ppermute x3, starting transfers between devices, sum_aux(): lax.ppermute(x, 'aux', [(i, i ^ shift) for i in range(n_aux)])  5.33 us
    ppermute x1, waiting for transfers between devices, columns_of(): lax.ppermute(held, 'pts', [(i, (i + shift) % n_pts) for i in range(n_pts)])  2.72 us
    pallas_call x1, Pallas kernels, load(): pl.pallas_call(load_kernel, in_specs=[ANY, ANY], out_specs=[VMEM] * 3, sc...  2.58 us
    ppermute x1, starting transfers between devices, columns_of(): lax.ppermute(held, 'pts', [(i, (i + shift) % n_pts) for i in range(n_pts)])  1.62 us
    pallas_call x1, Pallas kernels, first_rows(): pl.pallas_call(first_kernel, in_specs=[ANY], out_specs=VMEM, scratch_shap...  1.38 us
  transfers between devices with their start and end apart: 8, of which 4 were waited for; matrix products, arithmetic and copies ran while one was open for 0% of the time, Pallas kernels for 40%

profile of v3, /device:TPU:0, one launch (start us, length us, event | category | flops | bytes accessed | tf_op | source)
XLA Modules:
  0.0 51.3 jit_solution(16468404746405180076)
XLA Ops:
  0.0 0.0 copy-start
  0.0 1.4 %first_rows.1.sent = bf16[256,2048]{1,0:T(8,128)(2,1)S(1)} custom-call(bf16[512,4096]{1,0:T(8,128)(2,1)} %c_hbm.3), custom_call_target="tpu_custom_call" | custom-call | tf_op jit(solution)/shard_map/first_rows/pallas_call | solution.py:83
  1.4 0.5 %collective-permute-start.1 = (bf16[256,2048]{1,0:T(8,128)(2,1)S(1)}, bf16[256,2048]{1,0:T(8,128)(2,1)S(1)}, u32[]{:S(2)}, u32[]{:S(2)}) collective-permute-start(bf16[256,2048]{1,0:T(8,128)(2,1)S(1)} %first_rows.1.sent), channel_id=1, source_target_pairs={{0,1},{1,0},{2,3},{3,2},{4,5},{5,4},{6,7},{7,6},{8,9},{9,8},{10,11... | collective-permute-start | bytes 3145736 | tf_op jit(solution)/shard_map/ppermute | solution.py:195
  1.9 2.6 %load.1 = (bf16[512,2048]{1,0:T(8,128)(2,1)S(1)}, bf16[512,2048]{1,0:T(8,128)(2,1)S(1)}, bf16[256,2048]{1,0:T(8,128)(2,1)S(1)}) custom-call(bf16[512,4096]{1,0:T(8,128)(2,1)} %c_hbm.3, bf16[256,2048]{1,0:T(8,128)(2,1)S(1)} %first_rows.1.sent), custom_call_target="tpu_custom_call" | custom-call | bytes 4194304 | tf_op jit(solution)/shard_map/load/pallas_call | solution.py:97
  4.5 0.2 collective-permute-start
  4.7 0.0 collective-permute-done.1.far_ref
  4.7 0.0 copy-done
  4.7 8.9 %weights.3 = f32[2,16,1024]{2,1,0:T(8,128)S(1)} custom-call(bf16[16,256,512]{2,1,0:T(8,128)(2,1)S(1)} %copy-done, bf16[512,2048]{1,0:T(8,128)(2,1)S(1)} %get-tuple-element.10.c_ref, bf16[256,2048]{1,0:T(8,128)(2,1)S(1)} %collective-permute-done.1.far_ref), custom_call_target="tpu_custom_call" | custom-call | flops 8589934592 | tf_op jit(solution)/shard_map/weights/pallas_call | solution.py:111
  13.6 0.5 collective-permute-start.2
  14.1 0.0 collective-permute-done.far_ref
  14.1 9.1 %weights.2 = f32[2,16,1024]{2,1,0:T(8,128)S(1)} custom-call(bf16[16,256,512]{2,1,0:T(8,128)(2,1)S(1)} %copy-done, bf16[512,2048]{1,0:T(8,128)(2,1)S(1)} %get-tuple-element.8.c_ref, bf16[256,2048]{1,0:T(8,128)(2,1)S(1)} %collective-permute-done.far_ref), custom_call_target="tpu_custom_call" | custom-call | flops 8589934592 | tf_op jit(solution)/shard_map/weights/pallas_call | solution.py:111
  23.2 0.0 collective-permute-done.2
  23.2 2.7 %collective-permute-start.5 = (f32[2,16,1024]{2,1,0:T(8,128)S(1)}, f32[2,16,1024]{2,1,0:T(8,128)S(1)}, u32[]{:S(2)}, u32[]{:S(2)}) collective-permute-start(f32[2,16,1024]{2,1,0:T(8,128)S(1)} %add.24), channel_id=1, source_target_pairs={{0,4},{4,0},{8,12},{12,8},{1,5},{5,1},{9,13},{13,9},{2,6},{6,2},{1... | collective-permute-start | bytes 393224 | tf_op jit(solution)/shard_map/ppermute | solution.py:201
  26.0 2.6 %collective-permute-start.4 = (f32[2,16,1024]{2,1,0:T(8,128)S(1)}, f32[2,16,1024]{2,1,0:T(8,128)S(1)}, u32[]{:S(2)}, u32[]{:S(2)}) collective-permute-start(f32[2,16,1024]{2,1,0:T(8,128)S(1)} %add.24), channel_id=1, source_target_pairs={{0,8},{4,12},{8,0},{12,4},{1,9},{5,13},{9,1},{13,5},{2,10},{6,14},... | collective-permute-start | bytes 393224 | tf_op jit(solution)/shard_map/ppermute | solution.py:201
  28.6 0.0 collective-permute-start.3
  28.6 3.7 %collective-permute-done.5 = f32[2,16,1024]{2,1,0:T(8,128)S(1)} collective-permute-done((f32[2,16,1024]{2,1,0:T(8,128)S(1)}, f32[2,16,1024]{2,1,0:T(8,128)S(1)}, u32[]{:S(2)}, u32[]{:S(2)}) %collective-permute-start.5) | collective-permute-done | bytes 131104 | tf_op jit(solution)/shard_map/ppermute | solution.py:201
  32.2 6.6 %collective-permute-done.4 = f32[2,16,1024]{2,1,0:T(8,128)S(1)} collective-permute-done((f32[2,16,1024]{2,1,0:T(8,128)S(1)}, f32[2,16,1024]{2,1,0:T(8,128)S(1)}, u32[]{:S(2)}, u32[]{:S(2)}) %collective-permute-start.4) | collective-permute-done | bytes 131104 | tf_op jit(solution)/shard_map/ppermute | solution.py:201
  38.9 0.0 collective-permute-done.3
  38.9 0.1 collective-permute-start.6
  39.0 1.3 %collective-permute-done.6.refs_1_ = f32[2,16,1024]{2,1,0:T(8,128)S(1)} collective-permute-done((f32[2,16,1024]{2,1,0:T(8,128)S(1)}, f32[2,16,1024]{2,1,0:T(8,128)S(1)}, u32[]{:S(2)}, u32[]{:S(2)}) %collective-permute-start.6) | collective-permute-done | bytes 131104 | tf_op jit(solution)/shard_map/ppermute | solution.py:195
  40.3 1.6 %collective-permute-start.7 = (f32[16,1024]{1,0:T(8,128)S(1)}, f32[16,1024]{1,0:T(8,128)S(1)}, u32[]{:S(2)}, u32[]{:S(2)}) collective-permute-start(f32[16,1024]{1,0:T(8,128)S(1)} %fusion), channel_id=1, source_target_pairs={{0,2},{2,0},{1,3},{3,1},{4,6},{6,4},{5,7},{7,5},{8,10},{10,8},{9,1... | collective-permute-start | bytes 196616 | tf_op jit(solution)/shard_map/ppermute | solution.py:232
  42.0 2.7 %collective-permute-done.7 = f32[16,1024]{1,0:T(8,128)S(1)} collective-permute-done((f32[16,1024]{1,0:T(8,128)S(1)}, f32[16,1024]{1,0:T(8,128)S(1)}, u32[]{:S(2)}, u32[]{:S(2)}) %collective-permute-start.7) | collective-permute-done | bytes 65568 | tf_op jit(solution)/shard_map/ppermute | solution.py:232
  44.7 6.4 %outer.1 = f32[4096,1024]{1,0:T(8,128)} custom-call(f32[2,16,1024]{2,1,0:T(8,128)S(1)} %add_add_fusion.refs_0_, f32[2,16,1024]{2,1,0:T(8,128)S(1)} %collective-permute-done.6.refs_1_, f32[16,1024]{1,0:T(8,128)S(1)} %broadcast_select_fusion.refs_2_), custom_call_target="tpu_custom_call" | custom-call | flops 805306368 | bytes 16777216 | tf_op jit(solution)/shard_map/outer/pallas_call | solution.py:179
  (4 shorter events, 0.1 us)
Async XLA Ops:
  0.0 4.7 %copy-start = (bf16[16,256,512]{2,1,0:T(8,128)(2,1)S(1)}, bf16[16,256,512]{2,1,0:T(8,128)(2,1)}, u32[]{:S(2)}) copy-start(bf16[16,256,512]{2,1,0:T(8,128)(2,1)} %d_ref.3) | copy-start | bytes 12582916
  1.4 3.3 %collective-permute-start.1 = (bf16[256,2048]{1,0:T(8,128)(2,1)S(1)}, bf16[256,2048]{1,0:T(8,128)(2,1)S(1)}, u32[]{:S(2)}, u32[]{:S(2)}) collective-permute-start(bf16[256,2048]{1,0:T(8,128)(2,1)S(1)} %first_rows.1.sent), channel_id=1, source_target_pairs={{0,1},{1,0},{2,3},{3,2},{4,5},{5,4},{6,7},{7,6},{8,9},{9,8},{10,11... | collective-permute-start | bytes 3145736 | tf_op jit(solution)/shard_map/ppermute | solution.py:195
  4.5 9.6 %collective-permute-start = (bf16[256,2048]{1,0:T(8,128)(2,1)S(1)}, bf16[256,2048]{1,0:T(8,128)(2,1)S(1)}, u32[]{:S(2)}, u32[]{:S(2)}) collective-permute-start(bf16[256,2048]{1,0:T(8,128)(2,1)S(1)} %get-tuple-element.9), channel_id=1, source_target_pairs={{0,1},{1,0},{2,3},{3,2},{4,5},{5,4},{6,7},{7,6},{8,9},{9,8},{10,11... | collective-permute-start | bytes 3145736 | tf_op jit(solution)/shard_map/ppermute | solution.py:195
  13.6 9.6 %collective-permute-start.2 = (f32[2,16,1024]{2,1,0:T(8,128)S(1)}, f32[2,16,1024]{2,1,0:T(8,128)S(1)}, u32[]{:S(2)}, u32[]{:S(2)}) collective-permute-start(f32[2,16,1024]{2,1,0:T(8,128)S(1)} %weights.3), channel_id=1, source_target_pairs={{0,1},{1,0},{2,3},{3,2},{4,5},{5,4},{6,7},{7,6},{8,9},{9,8},{10,11... | collective-permute-start | bytes 393224 | tf_op jit(solution)/shard_map/ppermute | solution.py:195
  23.2 9.0 %collective-permute-start.5 = (f32[2,16,1024]{2,1,0:T(8,128)S(1)}, f32[2,16,1024]{2,1,0:T(8,128)S(1)}, u32[]{:S(2)}, u32[]{:S(2)}) collective-permute-start(f32[2,16,1024]{2,1,0:T(8,128)S(1)} %add.24), channel_id=1, source_target_pairs={{0,4},{4,0},{8,12},{12,8},{1,5},{5,1},{9,13},{13,9},{2,6},{6,2},{1... | collective-permute-start | bytes 393224 | tf_op jit(solution)/shard_map/ppermute | solution.py:201
  26.0 12.9 %collective-permute-start.4 = (f32[2,16,1024]{2,1,0:T(8,128)S(1)}, f32[2,16,1024]{2,1,0:T(8,128)S(1)}, u32[]{:S(2)}, u32[]{:S(2)}) collective-permute-start(f32[2,16,1024]{2,1,0:T(8,128)S(1)} %add.24), channel_id=1, source_target_pairs={{0,8},{4,12},{8,0},{12,4},{1,9},{5,13},{9,1},{13,5},{2,10},{6,14},... | collective-permute-start | bytes 393224 | tf_op jit(solution)/shard_map/ppermute | solution.py:201
  28.6 10.3 %collective-permute-start.3 = (f32[2,16,1024]{2,1,0:T(8,128)S(1)}, f32[2,16,1024]{2,1,0:T(8,128)S(1)}, u32[]{:S(2)}, u32[]{:S(2)}) collective-permute-start(f32[2,16,1024]{2,1,0:T(8,128)S(1)} %add.24), channel_id=1, source_target_pairs={{0,12},{4,8},{8,4},{12,0},{1,13},{5,9},{9,5},{13,1},{2,14},{6,10},... | collective-permute-start | bytes 393224 | tf_op jit(solution)/shard_map/ppermute | solution.py:201
  38.9 1.4 %collective-permute-start.6 = (f32[2,16,1024]{2,1,0:T(8,128)S(1)}, f32[2,16,1024]{2,1,0:T(8,128)S(1)}, u32[]{:S(2)}, u32[]{:S(2)}) collective-permute-start(f32[2,16,1024]{2,1,0:T(8,128)S(1)} %add_add_fusion.refs_0_), channel_id=1, source_target_pairs={{0,1},{1,0},{2,3},{3,2},{4,5},{5,4},{6,7},{7,6},{8,9},{9,8},{10,11... | collective-permute-start | bytes 393224 | tf_op jit(solution)/shard_map/ppermute | solution.py:195
  40.3 4.3 %collective-permute-start.7 = (f32[16,1024]{1,0:T(8,128)S(1)}, f32[16,1024]{1,0:T(8,128)S(1)}, u32[]{:S(2)}, u32[]{:S(2)}) collective-permute-start(f32[16,1024]{1,0:T(8,128)S(1)} %fusion), channel_id=1, source_target_pairs={{0,2},{2,0},{1,3},{3,1},{4,6},{6,4},{5,7},{7,5},{8,10},{10,8},{9,1... | collective-permute-start | bytes 196616 | tf_op jit(solution)/shard_map/ppermute | solution.py:232

commit v4 on v3

--- a/solution.py
+++ b/solution.py
@@ -16,26 +16,30 @@
 TILE = 512
 
 
-def first_kernel(c_hbm, rows_ref, sem):
+def first_kernel(c_hbm, rows_ref, sems):
     depth, points = rows_ref.shape
     place = Place(depth, points)
-    copy = pltpu.make_async_copy(c_hbm.at[place.rows, place.quarter(1)], rows_ref, sem)
-    copy.start()
-    copy.wait()
+    copies = place.copies(1, c_hbm.at[place.rows], rows_ref, sems)
+    for copy in copies:
+        copy.start()
+    for copy in copies:
+        copy.wait()
 
 
 def load_kernel(c_hbm, sent, c_ref, next_ref, rows_ref, sems):
     depth, points = rows_ref.shape
     place = Place(depth, points)
-    copies = [
-        pltpu.make_async_copy(c_hbm.at[place.rows, place.quarter(0)], rows_ref, sems.at[0]),
-        pltpu.make_async_copy(c_hbm.at[:, place.quarter(0)], c_ref, sems.at[1]),
-        pltpu.make_async_copy(c_hbm.at[:, place.quarter(1)], next_ref, sems.at[2]),
-    ]
-    for copy in copies:
+    first = place.copies(0, c_hbm, c_ref, sems.at[pl.ds(0, 2)])
+    second = place.copies(1, c_hbm, next_ref, sems.at[pl.ds(2, 2)])
+    rows = pltpu.make_async_copy(c_ref.at[place.rows], rows_ref, sems.at[4])
+    for copy in first + second:
         copy.start()
-    for copy in copies:
-        copy.wait()
+    for copy in first:
+        copy.wait()
+    rows.start()
+    for copy in second:
+        copy.wait()
+    rows.wait()
 
 
 class Place:
@@ -45,10 +49,18 @@
         per_core = lax.axis_size("aux") // 2
         self.near = aux // per_core == self.core
         self.rows = pl.ds(pl.multiple_of(aux % per_core * depth, 16), depth)
-        self.points = points
-
-    def quarter(self, own):
-        return pl.ds(pl.multiple_of((self.core if own else 1 - self.core) * self.points, 128), self.points)
+        self.block = points // 2
+
+    def copies(self, own, source, target, sems):
+        core = self.core if own else 1 - self.core
+        return [
+            pltpu.make_async_copy(
+                source.at[:, pl.ds(pl.multiple_of((2 * i + core) * self.block, 128), self.block)],
+                target.at[:, pl.ds(i * self.block, self.block)],
+                sems.at[i],
+            )
+            for i in range(2)
+        ]
 
 
 def weights_kernel(own, chunks, tile, depth, d_ref, c_ref, far_ref, *refs):
@@ -84,7 +96,7 @@
         first_kernel,
         in_specs=[ANY],
         out_specs=VMEM,
-        scratch_shapes=[pltpu.SemaphoreType.DMA],
+        scratch_shapes=[pltpu.SemaphoreType.DMA((2,))],
         out_shape=jax.ShapeDtypeStruct((depth, orbitals.shape[1] // 2), jnp.bfloat16),
         compiler_params=limit(SLICE_MIB),
         name="first_rows",
@@ -98,7 +110,7 @@
         load_kernel,
         in_specs=[ANY, ANY],
         out_specs=[VMEM] * 3,
-        scratch_shapes=[pltpu.SemaphoreType.DMA((3,))],
+        scratch_shapes=[pltpu.SemaphoreType.DMA((5,))],
         out_shape=[part, part, jax.ShapeDtypeStruct((depth, points // 2), jnp.bfloat16)],
         compiler_params=limit(LOAD_MIB),
         cost_estimate=pl.CostEstimate(flops=0, bytes_accessed=2 * orbitals.size, transcendentals=0),
@@ -141,7 +153,7 @@
     copies = []
     row = 0
     core = lax.axis_index("rep")
-    for quarter, chunks in ((core, own), (1 - core, other)):
+    for side, chunks in ((core, own), (1 - core, other)):
         for half in range(2):
             start = 0
             for chunk in chunks:
@@ -153,7 +165,7 @@
                     buffer[row : row + step, :] = lax.dot_general(
                         left, right, (((0,), (0,)), ((), ())), preferred_element_type=jnp.float32
                     )
-                    to = pl.multiple_of((quarter * 2 + half) * block + start + lo, 8)
+                    to = pl.multiple_of((half * 2 + side) * block + start + lo, 8)
                     copy = pltpu.make_async_copy(
                         buffer.at[pl.ds(row, step)],
                         out_hbm.at[pl.ds(to, step), pl.ds(at, width)],
@@ -197,13 +209,14 @@
 
 def sum_aux(x, n_aux):
     total = x
-    for shift in range(n_aux - 1, 0, -1):
+    middle = n_aux // 2
+    for shift in [i for i in range(1, n_aux) if i != middle] + [middle]:
         total = total + lax.ppermute(x, "aux", [(i, i ^ shift) for i in range(n_aux)])
     return total
 
 
 def per_device(n_aux, n_pts, density_slab, orbitals):
-    aux, pts, core = lax.axis_index("aux"), lax.axis_index("pts"), lax.axis_index("rep")
+    aux, pts = lax.axis_index("aux"), lax.axis_index("pts")
     n_k, depth, q = density_slab.shape
     points = orbitals.shape[1]
     block = points // 4
@@ -219,11 +232,6 @@
     keeps = quarter_weights(True, chunks, depth, n_k, d_rows, c_second, far_second)
     total = sum_aux(keeps[0] + came[0], n_aux)
 
-    def gather(total):
-        other = swap(total)
-        held = jnp.where(aux % 2 == core, total, other)
-        return other, lax.dynamic_index_in_dim(held, core, 0, keepdims=False)
-
     home = n_aux // n_pts
 
     def columns_of(held):
@@ -233,8 +241,8 @@
             got = jnp.where((pts - aux // home) % n_pts == shift, came, got)
         return got
 
-    other, held = gather(total)
-    return outer([total], [other], columns_of(held), (points, block), 0)
+    held = lax.dynamic_index_in_dim(total, aux % 2, 0, keepdims=False)
+    return outer([total], [swap(total)], columns_of(held), (points, block), 0)
 
 
 def solution(mesh):

time: 51.4 us -> 48.9 us (0.951)
  waiting for transfers between devices: 14.3 us -> 12.2 us
    ppermute x4, waiting for transfers between devices: 1.32 us -> 0.01 us  [swap(): return lax.ppermute(x, 'rep', [(0, 1), (1, 0)])]
    ppermute x3, waiting for transfers between devices: 10.3 us -> 9.44 us  [sum_aux(): lax.ppermute(x, 'aux', [(i, i ^ shift) for i in range(n_aux)])]
  transfers between devices with their start and end apart: 8 -> 8, of which waited for: 4 -> 3; matrix products, arithmetic and copies ran while one was open for 0% -> 0% of each run, Pallas kernels for 40% -> 42%
where the time goes in v4:
time: 48.9 us; the launch traced here: 48.7 us
  Pallas kernels  28.1 us (57%)
  waiting for transfers between devices  12.2 us (25%)
  starting transfers between devices  8.15 us (17%)
    pallas_call x2, Pallas kernels, quarter_weights(): pl.pallas_call(functools.partial(weights_kernel, own, chunks, TILE, depth...  18 us
    ppermute x3, waiting for transfers between devices, sum_aux(): lax.ppermute(x, 'aux', [(i, i ^ shift) for i in range(n_aux)])  9.44 us
    pallas_call x1, Pallas kernels, outer(): pl.pallas_call(functools.partial(outer_kernel, 1.0 / n_k, at, len(own)),...  6.42 us
    ppermute x3, starting transfers between devices, sum_aux(): lax.ppermute(x, 'aux', [(i, i ^ shift) for i in range(n_aux)])  5.38 us
    ppermute x1, waiting for transfers between devices, columns_of(): lax.ppermute(held, 'pts', [(i, (i + shift) % n_pts) for i in range(n_pts)])  2.72 us
    pallas_call x1, Pallas kernels, load(): pl.pallas_call(load_kernel, in_specs=[ANY, ANY], out_specs=[VMEM] * 3, sc...  2.23 us
    ppermute x1, starting transfers between devices, columns_of(): lax.ppermute(held, 'pts', [(i, (i + shift) % n_pts) for i in range(n_pts)])  1.61 us
    pallas_call x1, Pallas kernels, first_rows(): pl.pallas_call(first_kernel, in_specs=[ANY], out_specs=VMEM, scratch_shap...  1.37 us
  transfers between devices with their start and end apart: 8, of which 3 were waited for; matrix products, arithmetic and copies ran while one was open for 0% of the time, Pallas kernels for 42%

profile of v4, /device:TPU:0, one launch (start us, length us, event | category | flops | bytes accessed | tf_op | source)
XLA Modules:
  0.0 48.7 jit_solution(5849053114797755787)
XLA Ops:
  0.0 0.0 copy-start
  0.0 1.4 %first_rows.1.sent = bf16[256,2048]{1,0:T(8,128)(2,1)S(1)} custom-call(bf16[512,4096]{1,0:T(8,128)(2,1)} %c_hbm.3), custom_call_target="tpu_custom_call" | custom-call | tf_op jit(solution)/shard_map/first_rows/pallas_call | solution.py:95
  1.4 0.5 %collective-permute-start.1 = (bf16[256,2048]{1,0:T(8,128)(2,1)S(1)}, bf16[256,2048]{1,0:T(8,128)(2,1)S(1)}, u32[]{:S(2)}, u32[]{:S(2)}) collective-permute-start(bf16[256,2048]{1,0:T(8,128)(2,1)S(1)} %first_rows.1.sent), channel_id=1, source_target_pairs={{0,1},{1,0},{2,3},{3,2},{4,5},{5,4},{6,7},{7,6},{8,9},{9,8},{10,11... | collective-permute-start | bytes 3145736 | tf_op jit(solution)/shard_map/ppermute | solution.py:207
  1.9 2.2 %load.1 = (bf16[512,2048]{1,0:T(8,128)(2,1)S(1)}, bf16[512,2048]{1,0:T(8,128)(2,1)S(1)}, bf16[256,2048]{1,0:T(8,128)(2,1)S(1)}) custom-call(bf16[512,4096]{1,0:T(8,128)(2,1)} %c_hbm.3, bf16[256,2048]{1,0:T(8,128)(2,1)S(1)} %first_rows.1.sent), custom_call_target="tpu_custom_call" | custom-call | bytes 4194304 | tf_op jit(solution)/shard_map/load/pallas_call | solution.py:109
  4.1 0.2 collective-permute-start
  4.3 0.0 collective-permute-done.1.far_ref
  4.3 0.0 copy-done
  4.3 8.9 %weights.3 = f32[2,16,1024]{2,1,0:T(8,128)S(1)} custom-call(bf16[16,256,512]{2,1,0:T(8,128)(2,1)S(1)} %copy-done, bf16[512,2048]{1,0:T(8,128)(2,1)S(1)} %get-tuple-element.10.c_ref, bf16[256,2048]{1,0:T(8,128)(2,1)S(1)} %collective-permute-done.1.far_ref), custom_call_target="tpu_custom_call" | custom-call | flops 8589934592 | tf_op jit(solution)/shard_map/weights/pallas_call | solution.py:123
  13.3 0.4 collective-permute-start.2
  13.7 0.0 collective-permute-done.far_ref
  13.7 9.1 %weights.2 = f32[2,16,1024]{2,1,0:T(8,128)S(1)} custom-call(bf16[16,256,512]{2,1,0:T(8,128)(2,1)S(1)} %copy-done, bf16[512,2048]{1,0:T(8,128)(2,1)S(1)} %get-tuple-element.8.c_ref, bf16[256,2048]{1,0:T(8,128)(2,1)S(1)} %collective-permute-done.far_ref), custom_call_target="tpu_custom_call" | custom-call | flops 8589934592 | tf_op jit(solution)/shard_map/weights/pallas_call | solution.py:123
  22.8 0.0 collective-permute-done.2
  22.9 3.8 %collective-permute-start.5 = (f32[2,16,1024]{2,1,0:T(8,128)S(1)}, f32[2,16,1024]{2,1,0:T(8,128)S(1)}, u32[]{:S(2)}, u32[]{:S(2)}) collective-permute-start(f32[2,16,1024]{2,1,0:T(8,128)S(1)} %add.24), channel_id=1, source_target_pairs={{0,8},{4,12},{8,0},{12,4},{1,9},{5,13},{9,1},{13,5},{2,10},{6,14},... | collective-permute-start | bytes 393224 | tf_op jit(solution)/shard_map/ppermute | solution.py:214
  26.7 1.3 %collective-permute-start.4 = (f32[2,16,1024]{2,1,0:T(8,128)S(1)}, f32[2,16,1024]{2,1,0:T(8,128)S(1)}, u32[]{:S(2)}, u32[]{:S(2)}) collective-permute-start(f32[2,16,1024]{2,1,0:T(8,128)S(1)} %add.24), channel_id=1, source_target_pairs={{0,12},{4,8},{8,4},{12,0},{1,13},{5,9},{9,5},{13,1},{2,14},{6,10},... | collective-permute-start | bytes 393224 | tf_op jit(solution)/shard_map/ppermute | solution.py:214
  28.0 0.2 collective-permute-start.3
  28.3 8.4 %collective-permute-done.5 = f32[2,16,1024]{2,1,0:T(8,128)S(1)} collective-permute-done((f32[2,16,1024]{2,1,0:T(8,128)S(1)}, f32[2,16,1024]{2,1,0:T(8,128)S(1)}, u32[]{:S(2)}, u32[]{:S(2)}) %collective-permute-start.5) | collective-permute-done | bytes 131104 | tf_op jit(solution)/shard_map/ppermute | solution.py:214
  36.7 0.0 collective-permute-done.4
  36.7 1.0 %collective-permute-done.3 = f32[2,16,1024]{2,1,0:T(8,128)S(1)} collective-permute-done((f32[2,16,1024]{2,1,0:T(8,128)S(1)}, f32[2,16,1024]{2,1,0:T(8,128)S(1)}, u32[]{:S(2)}, u32[]{:S(2)}) %collective-permute-start.3) | collective-permute-done | bytes 131104 | tf_op jit(solution)/shard_map/ppermute | solution.py:214
  37.8 1.6 %collective-permute-start.7 = (f32[16,1024]{1,0:T(8,128)S(1)}, f32[16,1024]{1,0:T(8,128)S(1)}, u32[]{:S(2)}, u32[]{:S(2)}) collective-permute-start(f32[16,1024]{1,0:T(8,128)S(1)} %dynamic-slice_bitcast_fusion), channel_id=1, source_target_pairs={{0,2},{2,0},{1,3},{3,1},{4,6},{6,4},{5,7},{7,5},{8,10},{10,8},{9,1... | collective-permute-start | bytes 196616 | tf_op jit(solution)/shard_map/ppermute | solution.py:240
  39.4 0.0 collective-permute-start.6
  39.4 2.7 %collective-permute-done.7 = f32[16,1024]{1,0:T(8,128)S(1)} collective-permute-done((f32[16,1024]{1,0:T(8,128)S(1)}, f32[16,1024]{1,0:T(8,128)S(1)}, u32[]{:S(2)}, u32[]{:S(2)}) %collective-permute-start.7) | collective-permute-done | bytes 65568 | tf_op jit(solution)/shard_map/ppermute | solution.py:240
  42.1 0.0 collective-permute-done.6.refs_1_
  42.1 6.4 %outer.1 = f32[4096,1024]{1,0:T(8,128)} custom-call(f32[2,16,1024]{2,1,0:T(8,128)S(1)} %add_add_fusion.refs_0_, f32[2,16,1024]{2,1,0:T(8,128)S(1)} %collective-permute-done.6.refs_1_, f32[16,1024]{1,0:T(8,128)S(1)} %broadcast_select_fusion.refs_2_), custom_call_target="tpu_custom_call" | custom-call | flops 805306368 | bytes 16777216 | tf_op jit(solution)/shard_map/outer/pallas_call | solution.py:191
  (4 shorter events, 0.1 us)
Async XLA Ops:
  0.0 4.3 %copy-start = (bf16[16,256,512]{2,1,0:T(8,128)(2,1)S(1)}, bf16[16,256,512]{2,1,0:T(8,128)(2,1)}, u32[]{:S(2)}) copy-start(bf16[16,256,512]{2,1,0:T(8,128)(2,1)} %d_ref.3) | copy-start | bytes 12582916
  1.4 3.0 %collective-permute-start.1 = (bf16[256,2048]{1,0:T(8,128)(2,1)S(1)}, bf16[256,2048]{1,0:T(8,128)(2,1)S(1)}, u32[]{:S(2)}, u32[]{:S(2)}) collective-permute-start(bf16[256,2048]{1,0:T(8,128)(2,1)S(1)} %first_rows.1.sent), channel_id=1, source_target_pairs={{0,1},{1,0},{2,3},{3,2},{4,5},{5,4},{6,7},{7,6},{8,9},{9,8},{10,11... | collective-permute-start | bytes 3145736 | tf_op jit(solution)/shard_map/ppermute | solution.py:207
  4.1 9.6 %collective-permute-start = (bf16[256,2048]{1,0:T(8,128)(2,1)S(1)}, bf16[256,2048]{1,0:T(8,128)(2,1)S(1)}, u32[]{:S(2)}, u32[]{:S(2)}) collective-permute-start(bf16[256,2048]{1,0:T(8,128)(2,1)S(1)} %get-tuple-element.9), channel_id=1, source_target_pairs={{0,1},{1,0},{2,3},{3,2},{4,5},{5,4},{6,7},{7,6},{8,9},{9,8},{10,11... | collective-permute-start | bytes 3145736 | tf_op jit(solution)/shard_map/ppermute | solution.py:207
  13.3 9.6 %collective-permute-start.2 = (f32[2,16,1024]{2,1,0:T(8,128)S(1)}, f32[2,16,1024]{2,1,0:T(8,128)S(1)}, u32[]{:S(2)}, u32[]{:S(2)}) collective-permute-start(f32[2,16,1024]{2,1,0:T(8,128)S(1)} %weights.3), channel_id=1, source_target_pairs={{0,1},{1,0},{2,3},{3,2},{4,5},{5,4},{6,7},{7,6},{8,9},{9,8},{10,11... | collective-permute-start | bytes 393224 | tf_op jit(solution)/shard_map/ppermute | solution.py:207
  22.9 13.8 %collective-permute-start.5 = (f32[2,16,1024]{2,1,0:T(8,128)S(1)}, f32[2,16,1024]{2,1,0:T(8,128)S(1)}, u32[]{:S(2)}, u32[]{:S(2)}) collective-permute-start(f32[2,16,1024]{2,1,0:T(8,128)S(1)} %add.24), channel_id=1, source_target_pairs={{0,8},{4,12},{8,0},{12,4},{1,9},{5,13},{9,1},{13,5},{2,10},{6,14},... | collective-permute-start | bytes 393224 | tf_op jit(solution)/shard_map/ppermute | solution.py:214
  26.7 10.0 %collective-permute-start.4 = (f32[2,16,1024]{2,1,0:T(8,128)S(1)}, f32[2,16,1024]{2,1,0:T(8,128)S(1)}, u32[]{:S(2)}, u32[]{:S(2)}) collective-permute-start(f32[2,16,1024]{2,1,0:T(8,128)S(1)} %add.24), channel_id=1, source_target_pairs={{0,12},{4,8},{8,4},{12,0},{1,13},{5,9},{9,5},{13,1},{2,14},{6,10},... | collective-permute-start | bytes 393224 | tf_op jit(solution)/shard_map/ppermute | solution.py:214
  28.0 9.7 %collective-permute-start.3 = (f32[2,16,1024]{2,1,0:T(8,128)S(1)}, f32[2,16,1024]{2,1,0:T(8,128)S(1)}, u32[]{:S(2)}, u32[]{:S(2)}) collective-permute-start(f32[2,16,1024]{2,1,0:T(8,128)S(1)} %add.24), channel_id=1, source_target_pairs={{0,4},{4,0},{8,12},{12,8},{1,5},{5,1},{9,13},{13,9},{2,6},{6,2},{1... | collective-permute-start | bytes 393224 | tf_op jit(solution)/shard_map/ppermute | solution.py:214
  37.8 4.3 %collective-permute-start.7 = (f32[16,1024]{1,0:T(8,128)S(1)}, f32[16,1024]{1,0:T(8,128)S(1)}, u32[]{:S(2)}, u32[]{:S(2)}) collective-permute-start(f32[16,1024]{1,0:T(8,128)S(1)} %dynamic-slice_bitcast_fusion), channel_id=1, source_target_pairs={{0,2},{2,0},{1,3},{3,1},{4,6},{6,4},{5,7},{7,5},{8,10},{10,8},{9,1... | collective-permute-start | bytes 196616 | tf_op jit(solution)/shard_map/ppermute | solution.py:240
  39.4 2.7 %collective-permute-start.6 = (f32[2,16,1024]{2,1,0:T(8,128)S(1)}, f32[2,16,1024]{2,1,0:T(8,128)S(1)}, u32[]{:S(2)}, u32[]{:S(2)}) collective-permute-start(f32[2,16,1024]{2,1,0:T(8,128)S(1)} %add_add_fusion.refs_0_), channel_id=1, source_target_pairs={{0,1},{1,0},{2,3},{3,2},{4,5},{5,4},{6,7},{7,6},{8,9},{9,8},{10,11... | collective-permute-start | bytes 393224 | tf_op jit(solution)/shard_map/ppermute | solution.py:207

commit v5 on v4

--- a/solution.py
+++ b/solution.py
@@ -49,13 +49,14 @@
         per_core = lax.axis_size("aux") // 2
         self.near = aux // per_core == self.core
         self.rows = pl.ds(pl.multiple_of(aux % per_core * depth, 16), depth)
+        self.parity = aux % 2
         self.block = points // 2
 
     def copies(self, own, source, target, sems):
         core = self.core if own else 1 - self.core
         return [
             pltpu.make_async_copy(
-                source.at[:, pl.ds(pl.multiple_of((2 * i + core) * self.block, 128), self.block)],
+                source.at[:, pl.ds(pl.multiple_of(((i + self.parity) % 2 * 2 + core) * self.block, 128), self.block)],
                 target.at[:, pl.ds(i * self.block, self.block)],
                 sems.at[i],
             )
@@ -69,16 +70,15 @@
     points = c_ref.shape[1]
     block = points // 2
     place = Place(depth, points)
-    outs = refs
-    for (start, width), w_ref in zip(chunks, outs):
-        for half in range(2):
+    for half, w_ref in enumerate(refs):
+        for start, width in chunks:
             for lo in range(0, width, tile):
                 size = min(tile, width - lo)
                 there = slice(half * block + start + lo, half * block + start + lo + size)
                 scale = jnp.where(place.near, c_ref[place.rows, there], far_ref[:, there]).astype(jnp.float32)
                 for g in range(n_groups):
                     product = jnp.dot(d_ref[g], c_ref[:, there], preferred_element_type=jnp.float32)
-                    w_ref[half, g * span : (g + 1) * span, lo : lo + size] = jnp.sum(
+                    w_ref[g * span : (g + 1) * span, lo : lo + size] = jnp.sum(
                         product.reshape(span, depth, size) * scale[None], axis=1
                     )
 
@@ -119,7 +119,7 @@
 
 
 def quarter_weights(own, chunks, depth, n_k, d_rows, c_part, far, *more):
-    outs = [jax.ShapeDtypeStruct((2, n_k, width), jnp.float32) for _, width in chunks]
+    outs = [jax.ShapeDtypeStruct((n_k, c_part.shape[1] // 2), jnp.float32)] * 2
     return pl.pallas_call(
         functools.partial(weights_kernel, own, chunks, TILE, depth),
         in_specs=[VMEM] * 3 + [ANY] * len(more),
@@ -142,77 +142,58 @@
     return high, middle, low
 
 
-def outer_kernel(scale, at, n_rows, *refs):
-    own, other, columns = refs[:n_rows], refs[n_rows : 2 * n_rows], refs[2 * n_rows]
-    out_hbm, buffer, sems = refs[-3:]
-    width = columns.shape[1]
-    block = sum(x.shape[2] for x in own)
-
+def outer_kernel(scale, *refs):
+    *rows, columns, out_hbm, buffer, sems = refs
+    core, parity = lax.axis_index("rep"), lax.axis_index("aux") % 2
     high, middle, low = split(columns[...] * scale)
     right = jnp.concatenate([high, middle, high, low, middle, high], axis=0)
     copies = []
-    row = 0
-    core = lax.axis_index("rep")
-    for side, chunks in ((core, own), (1 - core, other)):
-        for half in range(2):
-            start = 0
-            for chunk in chunks:
-                size = chunk.shape[2]
-                step = min(size, 384 if size % 384 == 0 else 256)
-                for lo in range(0, size, step):
-                    high, middle, low = split(chunk[half, :, lo : lo + step])
-                    left = jnp.concatenate([high, high, middle, high, middle, low], axis=0)
-                    buffer[row : row + step, :] = lax.dot_general(
-                        left, right, (((0,), (0,)), ((), ())), preferred_element_type=jnp.float32
-                    )
-                    to = pl.multiple_of((half * 2 + side) * block + start + lo, 8)
-                    copy = pltpu.make_async_copy(
-                        buffer.at[pl.ds(row, step)],
-                        out_hbm.at[pl.ds(to, step), pl.ds(at, width)],
-                        sems.at[len(copies)],
-                    )
-                    copy.start()
-                    copies.append(copy)
-                    row += step
-                start += size
+    for i, weights in enumerate(rows):
+        block = weights.shape[1]
+        half = 1 - parity if i % 2 else parity
+        side = 1 - core if i // 2 else core
+        step = min(block, ROWS)
+        for lo in range(0, block, step):
+            high, middle, low = split(weights[:, lo : lo + step])
+            left = jnp.concatenate([high, high, middle, high, middle, low], axis=0)
+            here = pl.ds(i * block + lo, step)
+            buffer[here, :] = lax.dot_general(
+                left, right, (((0,), (0,)), ((), ())), preferred_element_type=jnp.float32
+            )
+            to = pl.ds(pl.multiple_of((half * 2 + side) * block + lo, 8), step)
+            copy = pltpu.make_async_copy(buffer.at[here], out_hbm.at[to], sems.at[len(copies)])
+            copy.start()
+            copies.append(copy)
     for copy in copies:
         copy.wait()
 
 
-def outer(own, other, columns, out_shape, at, before=None):
+def outer(rows, columns, out_shape):
     n_k, width = columns.shape
-    args = [*own, *other, columns]
-    specs = [VMEM] * len(args)
-    aliases = {}
-    if before is not None:
-        aliases = {len(args): 0}
-        args.append(before)
-        specs.append(ANY)
-    return pl.pallas_call(
-        functools.partial(outer_kernel, 1.0 / n_k, at, len(own)),
-        in_specs=specs,
+    return pl.pallas_call(
+        functools.partial(outer_kernel, 1.0 / n_k),
+        in_specs=[VMEM] * (len(rows) + 1),
         out_specs=ANY,
-        scratch_shapes=[pltpu.VMEM((out_shape[0], width), jnp.float32), pltpu.SemaphoreType.DMA((32,))],
+        scratch_shapes=[pltpu.VMEM(out_shape, jnp.float32), pltpu.SemaphoreType.DMA((32,))],
         out_shape=jax.ShapeDtypeStruct(out_shape, jnp.float32),
-        input_output_aliases=aliases,
         compiler_params=limit(OUTER_MIB),
         cost_estimate=pl.CostEstimate(
             flops=2 * 6 * n_k * out_shape[0] * width, bytes_accessed=4 * out_shape[0] * width, transcendentals=0
         ),
         name="outer",
-    )(*args)
+    )(*rows, columns)
 
 
 def swap(x):
     return lax.ppermute(x, "rep", [(0, 1), (1, 0)])
 
 
-def sum_aux(x, n_aux):
-    total = x
+def from_aux(even, odd, n_aux):
     middle = n_aux // 2
-    for shift in [i for i in range(1, n_aux) if i != middle] + [middle]:
-        total = total + lax.ppermute(x, "aux", [(i, i ^ shift) for i in range(n_aux)])
-    return total
+    return [
+        lax.ppermute(odd if shift % 2 else even, "aux", [(i, i ^ shift) for i in range(n_aux)])
+        for shift in [middle] + [i for i in range(1, n_aux) if i != middle]
+    ]
 
 
 def per_device(n_aux, n_pts, density_slab, orbitals):
@@ -230,7 +211,11 @@
     sends = quarter_weights(False, chunks, depth, n_k, d_rows, c_first, far_first)
     came = [swap(x) for x in sends]
     keeps = quarter_weights(True, chunks, depth, n_k, d_rows, c_second, far_second)
-    total = sum_aux(keeps[0] + came[0], n_aux)
+    mine, cross = lax.optimization_barrier([x + y for x, y in zip(keeps, came)])
+
+    a_came = from_aux(mine, cross, n_aux)
+    b_came = from_aux(cross, mine, n_aux)
+    a_total = sum(a_came, mine)
 
     home = n_aux // n_pts
 
@@ -241,8 +226,10 @@
             got = jnp.where((pts - aux // home) % n_pts == shift, came, got)
         return got
 
-    held = lax.dynamic_index_in_dim(total, aux % 2, 0, keepdims=False)
-    return outer([total], [swap(total)], columns_of(held), (points, block), 0)
+    columns = columns_of(a_total)
+    b_total = sum(b_came, cross)
+    rows = [a_total, b_total, swap(a_total), swap(b_total)]
+    return outer(rows, columns, (points, block))
 
 
 def solution(mesh):

time: 48.9 us -> 47.3 us (0.967)
  waiting for transfers between devices: 12.2 us -> 5.52 us
  starting transfers between devices: 8.15 us -> 13.3 us
    ppermute x3 -> x6, waiting for transfers between devices: 9.44 us -> 4.29 us  [from_aux(): lax.ppermute(odd if shift % 2 else even, 'aux', [(i, i ^ shift) for i in...]
    ppermute x3 -> x6, starting transfers between devices: 5.38 us -> 9.99 us  [from_aux(): lax.ppermute(odd if shift % 2 else even, 'aux', [(i, i ^ shift) for i in...]
    ppermute x1, waiting for transfers between devices: 2.72 us -> 0.01 us  [columns_of(): lax.ppermute(held, 'pts', [(i, (i + shift) % n_pts) for i in range(n_pts)])]
    ppermute x4 -> x6, waiting for transfers between devices: 0.01 us -> 1.23 us  [swap(): return lax.ppermute(x, 'rep', [(0, 1), (1, 0)])]
    ppermute x4 -> x6, starting transfers between devices: 1.16 us -> 1.37 us  [swap(): return lax.ppermute(x, 'rep', [(0, 1), (1, 0)])]
  transfers between devices with their start and end apart: 8 -> 13, of which waited for: 3 -> 5; matrix products, arithmetic and copies ran while one was open for 0% -> 0% of each run, Pallas kernels for 42% -> 43%
where the time goes in v5:
time: 47.3 us; the launch traced here: 47.2 us
  Pallas kernels  28.1 us (59%)
  starting transfers between devices  13.3 us (28%)
  waiting for transfers between devices  5.52 us (12%)
    pallas_call x2, Pallas kernels, quarter_weights(): pl.pallas_call(functools.partial(weights_kernel, own, chunks, TILE, depth...  18 us
    ppermute x6, starting transfers between devices, from_aux(): lax.ppermute(odd if shift % 2 else even, 'aux', [(i, i ^ shift) for i in...  9.99 us
    pallas_call x1, Pallas kernels, outer(): pl.pallas_call(functools.partial(outer_kernel, 1.0 / n_k), in_specs=[VMEM...  6.42 us
    ppermute x6, waiting for transfers between devices, from_aux(): lax.ppermute(odd if shift % 2 else even, 'aux', [(i, i ^ shift) for i in...  4.29 us
    pallas_call x1, Pallas kernels, load(): pl.pallas_call(load_kernel, in_specs=[ANY, ANY], out_specs=[VMEM] * 3, sc...  2.23 us
    ppermute x1, starting transfers between devices, columns_of(): lax.ppermute(held, 'pts', [(i, (i + shift) % n_pts) for i in range(n_pts)])  1.94 us
    ppermute x6, starting transfers between devices, swap(): return lax.ppermute(x, 'rep', [(0, 1), (1, 0)])  1.37 us
    pallas_call x1, Pallas kernels, first_rows(): pl.pallas_call(first_kernel, in_specs=[ANY], out_specs=VMEM, scratch_shap...  1.37 us
  transfers between devices with their start and end apart: 13, of which 5 were waited for; matrix products, arithmetic and copies ran while one was open for 0% of the time, Pallas kernels for 43%

profile of v5, /device:TPU:0, one launch (start us, length us, event | category | flops | bytes accessed | tf_op | source)
XLA Modules:
  0.0 47.2 jit_solution(9718582235329900703)
XLA Ops:
  0.0 1.4 %first_rows.1.sent = bf16[256,2048]{1,0:T(8,128)(2,1)S(1)} custom-call(bf16[512,4096]{1,0:T(8,128)(2,1)} %c_hbm.3), custom_call_target="tpu_custom_call" | custom-call | tf_op jit(solution)/shard_map/first_rows/pallas_call | solution.py:95
  1.4 0.5 %collective-permute-start.1 = (bf16[256,2048]{1,0:T(8,128)(2,1)S(1)}, bf16[256,2048]{1,0:T(8,128)(2,1)S(1)}, u32[]{:S(2)}, u32[]{:S(2)}) collective-permute-start(bf16[256,2048]{1,0:T(8,128)(2,1)S(1)} %first_rows.1.sent), channel_id=1, source_target_pairs={{0,1},{1,0},{2,3},{3,2},{4,5},{5,4},{6,7},{7,6},{8,9},{9,8},{10,11... | collective-permute-start | bytes 3145736 | tf_op jit(solution)/shard_map/ppermute | solution.py:188
  1.9 2.2 %load.1 = (bf16[512,2048]{1,0:T(8,128)(2,1)S(1)}, bf16[512,2048]{1,0:T(8,128)(2,1)S(1)}, bf16[256,2048]{1,0:T(8,128)(2,1)S(1)}) custom-call(bf16[512,4096]{1,0:T(8,128)(2,1)} %c_hbm.3, bf16[256,2048]{1,0:T(8,128)(2,1)S(1)} %first_rows.1.sent), custom_call_target="tpu_custom_call" | custom-call | bytes 4194304 | tf_op jit(solution)/shard_map/load/pallas_call | solution.py:109
  4.1 0.2 collective-permute-start
  4.3 0.0 collective-permute-done.1.far_ref
  4.3 8.9 %weights.3 = (f32[16,1024]{1,0:T(8,128)S(1)}, f32[16,1024]{1,0:T(8,128)S(1)}) custom-call(bf16[16,256,512]{2,1,0:T(8,128)(2,1)S(1)} %copy-done, bf16[512,2048]{1,0:T(8,128)(2,1)S(1)} %get-tuple-element.17.c_ref, bf16[256,2048]{1,0:T(8,128)(2,1)S(1)} %collective-permute-done.1.far_ref), custom_call_target="tpu_custom_call" | custom-call | flops 8589934592 | tf_op jit(solution)/shard_map/weights/pallas_call | solution.py:123
  13.3 0.4 collective-permute-start.2
  13.7 0.1 collective-permute-start.3
  13.9 9.1 %weights.2 = (f32[16,1024]{1,0:T(8,128)S(1)}, f32[16,1024]{1,0:T(8,128)S(1)}) custom-call(bf16[16,256,512]{2,1,0:T(8,128)(2,1)S(1)} %copy-done, bf16[512,2048]{1,0:T(8,128)(2,1)S(1)} %get-tuple-element.14.c_ref, bf16[256,2048]{1,0:T(8,128)(2,1)S(1)} %collective-permute-done.far_ref), custom_call_target="tpu_custom_call" | custom-call | flops 8589934592 | tf_op jit(solution)/shard_map/weights/pallas_call | solution.py:123
  23.0 0.0 collective-permute-done.2
  23.0 4.0 %collective-permute-start.4 = (f32[16,1024]{1,0:T(8,128)S(1)}, f32[16,1024]{1,0:T(8,128)S(1)}, u32[]{:S(2)}, u32[]{:S(2)}) collective-permute-start(f32[16,1024]{1,0:T(8,128)S(1)} %add.29), channel_id=1, source_target_pairs={{0,8},{4,12},{8,0},{12,4},{1,9},{5,13},{9,1},{13,5},{2,10},{6,14},... | collective-permute-start | bytes 196616 | tf_op jit(solution)/shard_map/ppermute | solution.py:194
  27.1 1.3 %collective-permute-start.6 = (f32[16,1024]{1,0:T(8,128)S(1)}, f32[16,1024]{1,0:T(8,128)S(1)}, u32[]{:S(2)}, u32[]{:S(2)}) collective-permute-start(f32[16,1024]{1,0:T(8,128)S(1)} %add.30), channel_id=1, source_target_pairs={{0,12},{4,8},{8,4},{12,0},{1,13},{5,9},{9,5},{13,1},{2,14},{6,10},... | collective-permute-start | bytes 196616 | tf_op jit(solution)/shard_map/ppermute | solution.py:194
  28.4 0.2 collective-permute-start.5
  28.6 2.9 %collective-permute-start.9 = (f32[16,1024]{1,0:T(8,128)S(1)}, f32[16,1024]{1,0:T(8,128)S(1)}, u32[]{:S(2)}, u32[]{:S(2)}) collective-permute-start(f32[16,1024]{1,0:T(8,128)S(1)} %add.29), channel_id=1, source_target_pairs={{0,12},{4,8},{8,4},{12,0},{1,13},{5,9},{9,5},{13,1},{2,14},{6,10},... | collective-permute-start | bytes 196616 | tf_op jit(solution)/shard_map/ppermute | solution.py:194
  31.6 0.5 collective-permute-start.8
  32.0 1.0 %collective-permute-start.7 = (f32[16,1024]{1,0:T(8,128)S(1)}, f32[16,1024]{1,0:T(8,128)S(1)}, u32[]{:S(2)}, u32[]{:S(2)}) collective-permute-start(f32[16,1024]{1,0:T(8,128)S(1)} %add.30), channel_id=1, source_target_pairs={{0,8},{4,12},{8,0},{12,4},{1,9},{5,13},{9,1},{13,5},{2,10},{6,14},... | collective-permute-start | bytes 196616 | tf_op jit(solution)/shard_map/ppermute | solution.py:194
  33.0 0.9 %collective-permute-done.6 = f32[16,1024]{1,0:T(8,128)S(1)} collective-permute-done((f32[16,1024]{1,0:T(8,128)S(1)}, f32[16,1024]{1,0:T(8,128)S(1)}, u32[]{:S(2)}, u32[]{:S(2)}) %collective-permute-start.6) | collective-permute-done | bytes 65568 | tf_op jit(solution)/shard_map/ppermute | solution.py:194
  33.9 0.6 %collective-permute-done.5 = f32[16,1024]{1,0:T(8,128)S(1)} collective-permute-done((f32[16,1024]{1,0:T(8,128)S(1)}, f32[16,1024]{1,0:T(8,128)S(1)}, u32[]{:S(2)}, u32[]{:S(2)}) %collective-permute-start.5) | collective-permute-done | bytes 65568 | tf_op jit(solution)/shard_map/ppermute | solution.py:194
  34.5 1.9 %collective-permute-start.12 = (f32[16,1024]{1,0:T(8,128)S(1)}, f32[16,1024]{1,0:T(8,128)S(1)}, u32[]{:S(2)}, u32[]{:S(2)}) collective-permute-start(f32[16,1024]{1,0:T(8,128)S(1)} %add_add_fusion.1.refs_0_), channel_id=1, source_target_pairs={{0,2},{2,0},{1,3},{3,1},{4,6},{6,4},{5,7},{7,5},{8,10},{10,8},{9,1... | collective-permute-start | bytes 196616 | tf_op jit(solution)/shard_map/ppermute | solution.py:225
  36.4 0.8 %collective-permute-done.8 = f32[16,1024]{1,0:T(8,128)S(1)} collective-permute-done((f32[16,1024]{1,0:T(8,128)S(1)}, f32[16,1024]{1,0:T(8,128)S(1)}, u32[]{:S(2)}, u32[]{:S(2)}) %collective-permute-start.8) | collective-permute-done | bytes 65568 | tf_op jit(solution)/shard_map/ppermute | solution.py:194
  37.3 2.0 %collective-permute-done.7 = f32[16,1024]{1,0:T(8,128)S(1)} collective-permute-done((f32[16,1024]{1,0:T(8,128)S(1)}, f32[16,1024]{1,0:T(8,128)S(1)}, u32[]{:S(2)}, u32[]{:S(2)}) %collective-permute-start.7) | collective-permute-done | bytes 65568 | tf_op jit(solution)/shard_map/ppermute | solution.py:194
  39.3 0.1 collective-permute-start.11
  39.4 1.2 %collective-permute-done.11.refs_3_ = f32[16,1024]{1,0:T(8,128)S(1)} collective-permute-done((f32[16,1024]{1,0:T(8,128)S(1)}, f32[16,1024]{1,0:T(8,128)S(1)}, u32[]{:S(2)}, u32[]{:S(2)}) %collective-permute-start.11) | collective-permute-done | bytes 65568 | tf_op jit(solution)/shard_map/ppermute | solution.py:188
  40.6 6.4 %outer.1 = f32[4096,1024]{1,0:T(8,128)} custom-call(f32[16,1024]{1,0:T(8,128)S(1)} %add_add_fusion.1.refs_0_, f32[16,1024]{1,0:T(8,128)S(1)} %add_add_fusion.refs_1_, f32[16,1024]{1,0:T(8,128)S(1)} %collective-permute-done.10.refs_2_, f32[16,1024]{1,0:T(8,128)S(1)} %collective-permute-done.11.refs_3_, f32[16,1024]{1,0:T(8,128)S(1)} %broadcast_select_fusion.refs_4_), custom_call_target="tpu_custom_call" | custom-call | flops 805306368 | bytes 16777216 | tf_op jit(solution)/shard_map/outer/pallas_call | solution.py:173
  (14 shorter events, 0.1 us)
Async XLA Ops:
  0.0 4.3 %copy-start = (bf16[16,256,512]{2,1,0:T(8,128)(2,1)S(1)}, bf16[16,256,512]{2,1,0:T(8,128)(2,1)}, u32[]{:S(2)}) copy-start(bf16[16,256,512]{2,1,0:T(8,128)(2,1)} %d_ref.3) | copy-start | bytes 12582916
  1.4 3.0 %collective-permute-start.1 = (bf16[256,2048]{1,0:T(8,128)(2,1)S(1)}, bf16[256,2048]{1,0:T(8,128)(2,1)S(1)}, u32[]{:S(2)}, u32[]{:S(2)}) collective-permute-start(bf16[256,2048]{1,0:T(8,128)(2,1)S(1)} %first_rows.1.sent), channel_id=1, source_target_pairs={{0,1},{1,0},{2,3},{3,2},{4,5},{5,4},{6,7},{7,6},{8,9},{9,8},{10,11... | collective-permute-start | bytes 3145736 | tf_op jit(solution)/shard_map/ppermute | solution.py:188
  4.1 9.7 %collective-permute-start = (bf16[256,2048]{1,0:T(8,128)(2,1)S(1)}, bf16[256,2048]{1,0:T(8,128)(2,1)S(1)}, u32[]{:S(2)}, u32[]{:S(2)}) collective-permute-start(bf16[256,2048]{1,0:T(8,128)(2,1)S(1)} %get-tuple-element.15), channel_id=1, source_target_pairs={{0,1},{1,0},{2,3},{3,2},{4,5},{5,4},{6,7},{7,6},{8,9},{9,8},{10,11... | collective-permute-start | bytes 3145736 | tf_op jit(solution)/shard_map/ppermute | solution.py:188
  13.3 9.7 %collective-permute-start.2 = (f32[16,1024]{1,0:T(8,128)S(1)}, f32[16,1024]{1,0:T(8,128)S(1)}, u32[]{:S(2)}, u32[]{:S(2)}) collective-permute-start(f32[16,1024]{1,0:T(8,128)S(1)} %get-tuple-element.18), channel_id=1, source_target_pairs={{0,1},{1,0},{2,3},{3,2},{4,5},{5,4},{6,7},{7,6},{8,9},{9,8},{10,11... | collective-permute-start | bytes 196616 | tf_op jit(solution)/shard_map/ppermute | solution.py:188
  13.7 9.3 %collective-permute-start.3 = (f32[16,1024]{1,0:T(8,128)S(1)}, f32[16,1024]{1,0:T(8,128)S(1)}, u32[]{:S(2)}, u32[]{:S(2)}) collective-permute-start(f32[16,1024]{1,0:T(8,128)S(1)} %get-tuple-element.20), channel_id=1, source_target_pairs={{0,1},{1,0},{2,3},{3,2},{4,5},{5,4},{6,7},{7,6},{8,9},{9,8},{10,11... | collective-permute-start | bytes 196616 | tf_op jit(solution)/shard_map/ppermute | solution.py:188
  23.0 9.0 %collective-permute-start.4 = (f32[16,1024]{1,0:T(8,128)S(1)}, f32[16,1024]{1,0:T(8,128)S(1)}, u32[]{:S(2)}, u32[]{:S(2)}) collective-permute-start(f32[16,1024]{1,0:T(8,128)S(1)} %add.29), channel_id=1, source_target_pairs={{0,8},{4,12},{8,0},{12,4},{1,9},{5,13},{9,1},{13,5},{2,10},{6,14},... | collective-permute-start | bytes 196616 | tf_op jit(solution)/shard_map/ppermute | solution.py:194
  27.1 6.9 %collective-permute-start.6 = (f32[16,1024]{1,0:T(8,128)S(1)}, f32[16,1024]{1,0:T(8,128)S(1)}, u32[]{:S(2)}, u32[]{:S(2)}) collective-permute-start(f32[16,1024]{1,0:T(8,128)S(1)} %add.30), channel_id=1, source_target_pairs={{0,12},{4,8},{8,4},{12,0},{1,13},{5,9},{9,5},{13,1},{2,14},{6,10},... | collective-permute-start | bytes 196616 | tf_op jit(solution)/shard_map/ppermute | solution.py:194
  28.4 6.1 %collective-permute-start.5 = (f32[16,1024]{1,0:T(8,128)S(1)}, f32[16,1024]{1,0:T(8,128)S(1)}, u32[]{:S(2)}, u32[]{:S(2)}) collective-permute-start(f32[16,1024]{1,0:T(8,128)S(1)} %add.30), channel_id=1, source_target_pairs={{0,4},{4,0},{8,12},{12,8},{1,5},{5,1},{9,13},{13,9},{2,6},{6,2},{1... | collective-permute-start | bytes 196616 | tf_op jit(solution)/shard_map/ppermute | solution.py:194
  28.6 7.8 %collective-permute-start.9 = (f32[16,1024]{1,0:T(8,128)S(1)}, f32[16,1024]{1,0:T(8,128)S(1)}, u32[]{:S(2)}, u32[]{:S(2)}) collective-permute-start(f32[16,1024]{1,0:T(8,128)S(1)} %add.29), channel_id=1, source_target_pairs={{0,12},{4,8},{8,4},{12,0},{1,13},{5,9},{9,5},{13,1},{2,14},{6,10},... | collective-permute-start | bytes 196616 | tf_op jit(solution)/shard_map/ppermute | solution.py:194
  31.6 5.7 %collective-permute-start.8 = (f32[16,1024]{1,0:T(8,128)S(1)}, f32[16,1024]{1,0:T(8,128)S(1)}, u32[]{:S(2)}, u32[]{:S(2)}) collective-permute-start(f32[16,1024]{1,0:T(8,128)S(1)} %add.29), channel_id=1, source_target_pairs={{0,4},{4,0},{8,12},{12,8},{1,5},{5,1},{9,13},{13,9},{2,6},{6,2},{1... | collective-permute-start | bytes 196616 | tf_op jit(solution)/shard_map/ppermute | solution.py:194
  32.0 7.3 %collective-permute-start.7 = (f32[16,1024]{1,0:T(8,128)S(1)}, f32[16,1024]{1,0:T(8,128)S(1)}, u32[]{:S(2)}, u32[]{:S(2)}) collective-permute-start(f32[16,1024]{1,0:T(8,128)S(1)} %add.30), channel_id=1, source_target_pairs={{0,8},{4,12},{8,0},{12,4},{1,9},{5,13},{9,1},{13,5},{2,10},{6,14},... | collective-permute-start | bytes 196616 | tf_op jit(solution)/shard_map/ppermute | solution.py:194
  34.5 4.9 %collective-permute-start.12 = (f32[16,1024]{1,0:T(8,128)S(1)}, f32[16,1024]{1,0:T(8,128)S(1)}, u32[]{:S(2)}, u32[]{:S(2)}) collective-permute-start(f32[16,1024]{1,0:T(8,128)S(1)} %add_add_fusion.1.refs_0_), channel_id=1, source_target_pairs={{0,2},{2,0},{1,3},{3,1},{4,6},{6,4},{5,7},{7,5},{8,10},{10,8},{9,1... | collective-permute-start | bytes 196616 | tf_op jit(solution)/shard_map/ppermute | solution.py:225
  36.4 4.2 %collective-permute-start.10 = (f32[16,1024]{1,0:T(8,128)S(1)}, f32[16,1024]{1,0:T(8,128)S(1)}, u32[]{:S(2)}, u32[]{:S(2)}) collective-permute-start(f32[16,1024]{1,0:T(8,128)S(1)} %add_add_fusion.1.refs_0_), channel_id=1, source_target_pairs={{0,1},{1,0},{2,3},{3,2},{4,5},{5,4},{6,7},{7,6},{8,9},{9,8},{10,11... | collective-permute-start | bytes 196616 | tf_op jit(solution)/shard_map/ppermute | solution.py:188
  39.3 1.3 %collective-permute-start.11 = (f32[16,1024]{1,0:T(8,128)S(1)}, f32[16,1024]{1,0:T(8,128)S(1)}, u32[]{:S(2)}, u32[]{:S(2)}) collective-permute-start(f32[16,1024]{1,0:T(8,128)S(1)} %add_add_fusion.refs_1_), channel_id=1, source_target_pairs={{0,1},{1,0},{2,3},{3,2},{4,5},{5,4},{6,7},{7,6},{8,9},{9,8},{10,11... | collective-permute-start | bytes 196616 | tf_op jit(solution)/shard_map/ppermute | solution.py:188

commit v6 on v5

--- a/solution.py
+++ b/solution.py
@@ -188,12 +188,8 @@
     return lax.ppermute(x, "rep", [(0, 1), (1, 0)])
 
 
-def from_aux(even, odd, n_aux):
-    middle = n_aux // 2
-    return [
-        lax.ppermute(odd if shift % 2 else even, "aux", [(i, i ^ shift) for i in range(n_aux)])
-        for shift in [middle] + [i for i in range(1, n_aux) if i != middle]
-    ]
+def from_aux(x, n_aux, shift):
+    return lax.ppermute(x, "aux", [(i, i ^ shift) for i in range(n_aux)])
 
 
 def per_device(n_aux, n_pts, density_slab, orbitals):
@@ -213,9 +209,14 @@
     keeps = quarter_weights(True, chunks, depth, n_k, d_rows, c_second, far_second)
     mine, cross = lax.optimization_barrier([x + y for x, y in zip(keeps, came)])
 
-    a_came = from_aux(mine, cross, n_aux)
-    b_came = from_aux(cross, mine, n_aux)
-    a_total = sum(a_came, mine)
+    a_total = mine
+    for shift in [n_aux // 2] + [i for i in range(1, n_aux) if i != n_aux // 2]:
+        a_total = a_total + from_aux(cross if shift % 2 else mine, n_aux, shift)
+    b_total = cross + from_aux(mine, n_aux, 1)
+    shift = 2
+    while shift < n_aux:
+        b_total = b_total + from_aux(b_total, n_aux, shift)
+        shift *= 2
 
     home = n_aux // n_pts
 
@@ -227,7 +228,6 @@
         return got
 
     columns = columns_of(a_total)
-    b_total = sum(b_came, cross)
     rows = [a_total, b_total, swap(a_total), swap(b_total)]
     return outer(rows, columns, (points, block))
 

time: 47.3 us -> 46.6 us (0.985)
    ppermute x1, waiting for transfers between devices: 0.01 us -> 1.89 us  [columns_of(): lax.ppermute(held, 'pts', [(i, (i + shift) % n_pts) for i in range(n_pts)])]
    ppermute x6, waiting for transfers between devices: 1.23 us -> 0.02 us  [swap(): return lax.ppermute(x, 'rep', [(0, 1), (1, 0)])]
    ppermute x6 -> x5, waiting for transfers between devices: 4.29 us -> 3.21 us  [from_aux(): return lax.ppermute(x, 'aux', [(i, i ^ shift) for i in range(n_aux)])]
    ppermute x6 -> x5, starting transfers between devices: 9.99 us -> 10.1 us  [from_aux(): return lax.ppermute(x, 'aux', [(i, i ^ shift) for i in range(n_aux)])]
  transfers between devices with their start and end apart: 13 -> 12, of which waited for: 5 -> 4; matrix products, arithmetic and copies ran while one was open for 0% -> 0% of each run, Pallas kernels for 43% -> 44%
where the time goes in v6:
time: 46.6 us; the launch traced here: 46.5 us
  Pallas kernels  28.1 us (60%)
  starting transfers between devices  13 us (28%)
  waiting for transfers between devices  5.12 us (11%)
    pallas_call x2, Pallas kernels, quarter_weights(): pl.pallas_call(functools.partial(weights_kernel, own, chunks, TILE, depth...  18 us
    ppermute x5, starting transfers between devices, from_aux(): return lax.ppermute(x, 'aux', [(i, i ^ shift) for i in range(n_aux)])  10.1 us
    pallas_call x1, Pallas kernels, outer(): pl.pallas_call(functools.partial(outer_kernel, 1.0 / n_k), in_specs=[VMEM...  6.42 us
    ppermute x5, waiting for transfers between devices, from_aux(): return lax.ppermute(x, 'aux', [(i, i ^ shift) for i in range(n_aux)])  3.21 us
    pallas_call x1, Pallas kernels, load(): pl.pallas_call(load_kernel, in_specs=[ANY, ANY], out_specs=[VMEM] * 3, sc...  2.23 us
    ppermute x1, waiting for transfers between devices, columns_of(): lax.ppermute(held, 'pts', [(i, (i + shift) % n_pts) for i in range(n_pts)])  1.89 us
    ppermute x1, starting transfers between devices, columns_of(): lax.ppermute(held, 'pts', [(i, (i + shift) % n_pts) for i in range(n_pts)])  1.55 us
    ppermute x6, starting transfers between devices, swap(): return lax.ppermute(x, 'rep', [(0, 1), (1, 0)])  1.37 us
  transfers between devices with their start and end apart: 12, of which 4 were waited for; matrix products, arithmetic and copies ran while one was open for 0% of the time, Pallas kernels for 44%

profile of v6, /device:TPU:0, one launch (start us, length us, event | category | flops | bytes accessed | tf_op | source)
XLA Modules:
  0.0 46.5 jit_solution(13498117118336993542)
XLA Ops:
  0.0 1.4 %first_rows.1.sent = bf16[256,2048]{1,0:T(8,128)(2,1)S(1)} custom-call(bf16[512,4096]{1,0:T(8,128)(2,1)} %c_hbm.3), custom_call_target="tpu_custom_call" | custom-call | tf_op jit(solution)/shard_map/first_rows/pallas_call | solution.py:95
  1.4 0.5 %collective-permute-start.1 = (bf16[256,2048]{1,0:T(8,128)(2,1)S(1)}, bf16[256,2048]{1,0:T(8,128)(2,1)S(1)}, u32[]{:S(2)}, u32[]{:S(2)}) collective-permute-start(bf16[256,2048]{1,0:T(8,128)(2,1)S(1)} %first_rows.1.sent), channel_id=1, source_target_pairs={{0,1},{1,0},{2,3},{3,2},{4,5},{5,4},{6,7},{7,6},{8,9},{9,8},{10,11... | collective-permute-start | bytes 3145736 | tf_op jit(solution)/shard_map/ppermute | solution.py:188
  1.9 2.2 %load.1 = (bf16[512,2048]{1,0:T(8,128)(2,1)S(1)}, bf16[512,2048]{1,0:T(8,128)(2,1)S(1)}, bf16[256,2048]{1,0:T(8,128)(2,1)S(1)}) custom-call(bf16[512,4096]{1,0:T(8,128)(2,1)} %c_hbm.3, bf16[256,2048]{1,0:T(8,128)(2,1)S(1)} %first_rows.1.sent), custom_call_target="tpu_custom_call" | custom-call | bytes 4194304 | tf_op jit(solution)/shard_map/load/pallas_call | solution.py:109
  4.1 0.2 collective-permute-start
  4.3 0.0 collective-permute-done.1.far_ref
  4.3 8.9 %weights.3 = (f32[16,1024]{1,0:T(8,128)S(1)}, f32[16,1024]{1,0:T(8,128)S(1)}) custom-call(bf16[16,256,512]{2,1,0:T(8,128)(2,1)S(1)} %copy-done, bf16[512,2048]{1,0:T(8,128)(2,1)S(1)} %get-tuple-element.17.c_ref, bf16[256,2048]{1,0:T(8,128)(2,1)S(1)} %collective-permute-done.1.far_ref), custom_call_target="tpu_custom_call" | custom-call | flops 8589934592 | tf_op jit(solution)/shard_map/weights/pallas_call | solution.py:123
  13.3 0.4 collective-permute-start.2
  13.7 0.1 collective-permute-start.3
  13.8 0.0 collective-permute-done.far_ref
  13.9 9.1 %weights.2 = (f32[16,1024]{1,0:T(8,128)S(1)}, f32[16,1024]{1,0:T(8,128)S(1)}) custom-call(bf16[16,256,512]{2,1,0:T(8,128)(2,1)S(1)} %copy-done, bf16[512,2048]{1,0:T(8,128)(2,1)S(1)} %get-tuple-element.14.c_ref, bf16[256,2048]{1,0:T(8,128)(2,1)S(1)} %collective-permute-done.far_ref), custom_call_target="tpu_custom_call" | custom-call | flops 8589934592 | tf_op jit(solution)/shard_map/weights/pallas_call | solution.py:123
  23.0 0.0 collective-permute-done.2
  23.0 3.0 %collective-permute-start.7 = (f32[16,1024]{1,0:T(8,128)S(1)}, f32[16,1024]{1,0:T(8,128)S(1)}, u32[]{:S(2)}, u32[]{:S(2)}) collective-permute-start(f32[16,1024]{1,0:T(8,128)S(1)} %add.26), channel_id=1, source_target_pairs={{0,4},{4,0},{8,12},{12,8},{1,5},{5,1},{9,13},{13,9},{2,6},{6,2},{1... | collective-permute-start | bytes 196616 | tf_op jit(solution)/shard_map/ppermute | solution.py:192
  26.0 2.6 %collective-permute-start.4 = (f32[16,1024]{1,0:T(8,128)S(1)}, f32[16,1024]{1,0:T(8,128)S(1)}, u32[]{:S(2)}, u32[]{:S(2)}) collective-permute-start(f32[16,1024]{1,0:T(8,128)S(1)} %add.26), channel_id=1, source_target_pairs={{0,8},{4,12},{8,0},{12,4},{1,9},{5,13},{9,1},{13,5},{2,10},{6,14},... | collective-permute-start | bytes 196616 | tf_op jit(solution)/shard_map/ppermute | solution.py:192
  28.6 0.0 collective-permute-start.6
  28.6 0.9 %collective-permute-start.5 = (f32[16,1024]{1,0:T(8,128)S(1)}, f32[16,1024]{1,0:T(8,128)S(1)}, u32[]{:S(2)}, u32[]{:S(2)}) collective-permute-start(f32[16,1024]{1,0:T(8,128)S(1)} %add.27), channel_id=1, source_target_pairs={{0,4},{4,0},{8,12},{12,8},{1,5},{5,1},{9,13},{13,9},{2,6},{6,2},{1... | collective-permute-start | bytes 196616 | tf_op jit(solution)/shard_map/ppermute | solution.py:192
  29.5 0.0 collective-permute-done.7
  29.5 3.6 %collective-permute-start.8 = (f32[16,1024]{1,0:T(8,128)S(1)}, f32[16,1024]{1,0:T(8,128)S(1)}, u32[]{:S(2)}, u32[]{:S(2)}) collective-permute-start(f32[16,1024]{1,0:T(8,128)S(1)} %add.31), channel_id=1, source_target_pairs={{0,8},{4,12},{8,0},{12,4},{1,9},{5,13},{9,1},{13,5},{2,10},{6,14},... | collective-permute-start | bytes 196616 | tf_op jit(solution)/shard_map/ppermute | solution.py:192
  33.1 0.5 %collective-permute-done.4 = f32[16,1024]{1,0:T(8,128)S(1)} collective-permute-done((f32[16,1024]{1,0:T(8,128)S(1)}, f32[16,1024]{1,0:T(8,128)S(1)}, u32[]{:S(2)}, u32[]{:S(2)}) %collective-permute-start.4) | collective-permute-done | bytes 65568 | tf_op jit(solution)/shard_map/ppermute | solution.py:192
  33.6 1.9 %collective-permute-done.6 = f32[16,1024]{1,0:T(8,128)S(1)} collective-permute-done((f32[16,1024]{1,0:T(8,128)S(1)}, f32[16,1024]{1,0:T(8,128)S(1)}, u32[]{:S(2)}, u32[]{:S(2)}) %collective-permute-start.6) | collective-permute-done | bytes 65568 | tf_op jit(solution)/shard_map/ppermute | solution.py:192
  35.5 1.6 %collective-permute-start.11 = (f32[16,1024]{1,0:T(8,128)S(1)}, f32[16,1024]{1,0:T(8,128)S(1)}, u32[]{:S(2)}, u32[]{:S(2)}) collective-permute-start(f32[16,1024]{1,0:T(8,128)S(1)} %add_add_fusion.refs_0_), channel_id=1, source_target_pairs={{0,2},{2,0},{1,3},{3,1},{4,6},{6,4},{5,7},{7,5},{8,10},{10,8},{9,1... | collective-permute-start | bytes 196616 | tf_op jit(solution)/shard_map/ppermute | solution.py:226
  37.1 0.8 %collective-permute-done.8 = f32[16,1024]{1,0:T(8,128)S(1)} collective-permute-done((f32[16,1024]{1,0:T(8,128)S(1)}, f32[16,1024]{1,0:T(8,128)S(1)}, u32[]{:S(2)}, u32[]{:S(2)}) %collective-permute-start.8) | collective-permute-done | bytes 65568 | tf_op jit(solution)/shard_map/ppermute | solution.py:192
  37.9 0.1 collective-permute-start.10
  38.0 1.9 %collective-permute-done.11 = f32[16,1024]{1,0:T(8,128)S(1)} collective-permute-done((f32[16,1024]{1,0:T(8,128)S(1)}, f32[16,1024]{1,0:T(8,128)S(1)}, u32[]{:S(2)}, u32[]{:S(2)}) %collective-permute-start.11) | collective-permute-done | bytes 65568 | tf_op jit(solution)/shard_map/ppermute | solution.py:226
  39.9 6.4 %outer.1 = f32[4096,1024]{1,0:T(8,128)} custom-call(f32[16,1024]{1,0:T(8,128)S(1)} %add_add_fusion.refs_0_, f32[16,1024]{1,0:T(8,128)S(1)} %add.32.refs_1_, f32[16,1024]{1,0:T(8,128)S(1)} %collective-permute-done.9.refs_2_, f32[16,1024]{1,0:T(8,128)S(1)} %collective-permute-done.10.refs_3_, f32[16,1024]{1,0:T(8,128)S(1)} %broadcast_select_fusion.refs_4_), custom_call_target="tpu_custom_call" | custom-call | flops 805306368 | bytes 16777216 | tf_op jit(solution)/shard_map/outer/pallas_call | solution.py:173
  (13 shorter events, 0.1 us)
Async XLA Ops:
  0.0 4.3 %copy-start = (bf16[16,256,512]{2,1,0:T(8,128)(2,1)S(1)}, bf16[16,256,512]{2,1,0:T(8,128)(2,1)}, u32[]{:S(2)}) copy-start(bf16[16,256,512]{2,1,0:T(8,128)(2,1)} %d_ref.3) | copy-start | bytes 12582916
  1.4 3.0 %collective-permute-start.1 = (bf16[256,2048]{1,0:T(8,128)(2,1)S(1)}, bf16[256,2048]{1,0:T(8,128)(2,1)S(1)}, u32[]{:S(2)}, u32[]{:S(2)}) collective-permute-start(bf16[256,2048]{1,0:T(8,128)(2,1)S(1)} %first_rows.1.sent), channel_id=1, source_target_pairs={{0,1},{1,0},{2,3},{3,2},{4,5},{5,4},{6,7},{7,6},{8,9},{9,8},{10,11... | collective-permute-start | bytes 3145736 | tf_op jit(solution)/shard_map/ppermute | solution.py:188
  4.1 9.7 %collective-permute-start = (bf16[256,2048]{1,0:T(8,128)(2,1)S(1)}, bf16[256,2048]{1,0:T(8,128)(2,1)S(1)}, u32[]{:S(2)}, u32[]{:S(2)}) collective-permute-start(bf16[256,2048]{1,0:T(8,128)(2,1)S(1)} %get-tuple-element.15), channel_id=1, source_target_pairs={{0,1},{1,0},{2,3},{3,2},{4,5},{5,4},{6,7},{7,6},{8,9},{9,8},{10,11... | collective-permute-start | bytes 3145736 | tf_op jit(solution)/shard_map/ppermute | solution.py:188
  13.3 9.7 %collective-permute-start.2 = (f32[16,1024]{1,0:T(8,128)S(1)}, f32[16,1024]{1,0:T(8,128)S(1)}, u32[]{:S(2)}, u32[]{:S(2)}) collective-permute-start(f32[16,1024]{1,0:T(8,128)S(1)} %get-tuple-element.18), channel_id=1, source_target_pairs={{0,1},{1,0},{2,3},{3,2},{4,5},{5,4},{6,7},{7,6},{8,9},{9,8},{10,11... | collective-permute-start | bytes 196616 | tf_op jit(solution)/shard_map/ppermute | solution.py:188
  13.7 9.3 %collective-permute-start.3 = (f32[16,1024]{1,0:T(8,128)S(1)}, f32[16,1024]{1,0:T(8,128)S(1)}, u32[]{:S(2)}, u32[]{:S(2)}) collective-permute-start(f32[16,1024]{1,0:T(8,128)S(1)} %get-tuple-element.20), channel_id=1, source_target_pairs={{0,1},{1,0},{2,3},{3,2},{4,5},{5,4},{6,7},{7,6},{8,9},{9,8},{10,11... | collective-permute-start | bytes 196616 | tf_op jit(solution)/shard_map/ppermute | solution.py:188
  23.0 6.5 %collective-permute-start.7 = (f32[16,1024]{1,0:T(8,128)S(1)}, f32[16,1024]{1,0:T(8,128)S(1)}, u32[]{:S(2)}, u32[]{:S(2)}) collective-permute-start(f32[16,1024]{1,0:T(8,128)S(1)} %add.26), channel_id=1, source_target_pairs={{0,4},{4,0},{8,12},{12,8},{1,5},{5,1},{9,13},{13,9},{2,6},{6,2},{1... | collective-permute-start | bytes 196616 | tf_op jit(solution)/shard_map/ppermute | solution.py:192
  26.0 7.5 %collective-permute-start.4 = (f32[16,1024]{1,0:T(8,128)S(1)}, f32[16,1024]{1,0:T(8,128)S(1)}, u32[]{:S(2)}, u32[]{:S(2)}) collective-permute-start(f32[16,1024]{1,0:T(8,128)S(1)} %add.26), channel_id=1, source_target_pairs={{0,8},{4,12},{8,0},{12,4},{1,9},{5,13},{9,1},{13,5},{2,10},{6,14},... | collective-permute-start | bytes 196616 | tf_op jit(solution)/shard_map/ppermute | solution.py:192
  28.6 6.9 %collective-permute-start.6 = (f32[16,1024]{1,0:T(8,128)S(1)}, f32[16,1024]{1,0:T(8,128)S(1)}, u32[]{:S(2)}, u32[]{:S(2)}) collective-permute-start(f32[16,1024]{1,0:T(8,128)S(1)} %add.27), channel_id=1, source_target_pairs={{0,12},{4,8},{8,4},{12,0},{1,13},{5,9},{9,5},{13,1},{2,14},{6,10},... | collective-permute-start | bytes 196616 | tf_op jit(solution)/shard_map/ppermute | solution.py:192
  28.6 6.9 %collective-permute-start.5 = (f32[16,1024]{1,0:T(8,128)S(1)}, f32[16,1024]{1,0:T(8,128)S(1)}, u32[]{:S(2)}, u32[]{:S(2)}) collective-permute-start(f32[16,1024]{1,0:T(8,128)S(1)} %add.27), channel_id=1, source_target_pairs={{0,4},{4,0},{8,12},{12,8},{1,5},{5,1},{9,13},{13,9},{2,6},{6,2},{1... | collective-permute-start | bytes 196616 | tf_op jit(solution)/shard_map/ppermute | solution.py:192
  29.5 8.3 %collective-permute-start.8 = (f32[16,1024]{1,0:T(8,128)S(1)}, f32[16,1024]{1,0:T(8,128)S(1)}, u32[]{:S(2)}, u32[]{:S(2)}) collective-permute-start(f32[16,1024]{1,0:T(8,128)S(1)} %add.31), channel_id=1, source_target_pairs={{0,8},{4,12},{8,0},{12,4},{1,9},{5,13},{9,1},{13,5},{2,10},{6,14},... | collective-permute-start | bytes 196616 | tf_op jit(solution)/shard_map/ppermute | solution.py:192
  35.5 4.3 %collective-permute-start.11 = (f32[16,1024]{1,0:T(8,128)S(1)}, f32[16,1024]{1,0:T(8,128)S(1)}, u32[]{:S(2)}, u32[]{:S(2)}) collective-permute-start(f32[16,1024]{1,0:T(8,128)S(1)} %add_add_fusion.refs_0_), channel_id=1, source_target_pairs={{0,2},{2,0},{1,3},{3,1},{4,6},{6,4},{5,7},{7,5},{8,10},{10,8},{9,1... | collective-permute-start | bytes 196616 | tf_op jit(solution)/shard_map/ppermute | solution.py:226
  37.1 2.8 %collective-permute-start.9 = (f32[16,1024]{1,0:T(8,128)S(1)}, f32[16,1024]{1,0:T(8,128)S(1)}, u32[]{:S(2)}, u32[]{:S(2)}) collective-permute-start(f32[16,1024]{1,0:T(8,128)S(1)} %add_add_fusion.refs_0_), channel_id=1, source_target_pairs={{0,1},{1,0},{2,3},{3,2},{4,5},{5,4},{6,7},{7,6},{8,9},{9,8},{10,11... | collective-permute-start | bytes 196616 | tf_op jit(solution)/shard_map/ppermute | solution.py:188
  37.9 2.0 %collective-permute-start.10 = (f32[16,1024]{1,0:T(8,128)S(1)}, f32[16,1024]{1,0:T(8,128)S(1)}, u32[]{:S(2)}, u32[]{:S(2)}) collective-permute-start(f32[16,1024]{1,0:T(8,128)S(1)} %add.32.refs_1_), channel_id=1, source_target_pairs={{0,1},{1,0},{2,3},{3,2},{4,5},{5,4},{6,7},{7,6},{8,9},{9,8},{10,11... | collective-permute-start | bytes 196616 | tf_op jit(solution)/shard_map/ppermute | solution.py:188

commit v7 on v6

--- a/solution.py
+++ b/solution.py
@@ -152,8 +152,9 @@
         block = weights.shape[1]
         half = 1 - parity if i % 2 else parity
         side = 1 - core if i // 2 else core
-        step = min(block, ROWS)
-        for lo in range(0, block, step):
+        cuts = sorted({0, *([128] if i == 0 and block > 128 else []), *range(0, block, ROWS), block})
+        for lo, hi in zip(cuts, cuts[1:]):
+            step = hi - lo
             high, middle, low = split(weights[:, lo : lo + step])
             left = jnp.concatenate([high, high, middle, high, middle, low], axis=0)
             here = pl.ds(i * block + lo, step)

time: 46.6 us -> 46.6 us (level)
  no operation moved by 1% of the time
where the time goes in v7:
time: 46.6 us; the launch traced here: 46.4 us
  Pallas kernels  28 us (60%)
  starting transfers between devices  13 us (28%)
  waiting for transfers between devices  5.12 us (11%)
    pallas_call x2, Pallas kernels, quarter_weights(): pl.pallas_call(functools.partial(weights_kernel, own, chunks, TILE, depth...  18 us
    ppermute x5, starting transfers between devices, from_aux(): return lax.ppermute(x, 'aux', [(i, i ^ shift) for i in range(n_aux)])  10.1 us
    pallas_call x1, Pallas kernels, outer(): pl.pallas_call(functools.partial(outer_kernel, 1.0 / n_k), in_specs=[VMEM...  6.37 us
    ppermute x5, waiting for transfers between devices, from_aux(): return lax.ppermute(x, 'aux', [(i, i ^ shift) for i in range(n_aux)])  3.21 us
    pallas_call x1, Pallas kernels, load(): pl.pallas_call(load_kernel, in_specs=[ANY, ANY], out_specs=[VMEM] * 3, sc...  2.23 us
    ppermute x1, waiting for transfers between devices, columns_of(): lax.ppermute(held, 'pts', [(i, (i + shift) % n_pts) for i in range(n_pts)])  1.89 us
    ppermute x1, starting transfers between devices, columns_of(): lax.ppermute(held, 'pts', [(i, (i + shift) % n_pts) for i in range(n_pts)])  1.55 us
    ppermute x6, starting transfers between devices, swap(): return lax.ppermute(x, 'rep', [(0, 1), (1, 0)])  1.37 us
  transfers between devices with their start and end apart: 12, of which 4 were waited for; matrix products, arithmetic and copies ran while one was open for 0% of the time, Pallas kernels for 44%

profile of v7, /device:TPU:0, one launch (start us, length us, event | category | flops | bytes accessed | tf_op | source)
XLA Modules:
  0.0 46.4 jit_solution(7370151691294620586)
XLA Ops:
  0.0 1.4 %first_rows.1.sent = bf16[256,2048]{1,0:T(8,128)(2,1)S(1)} custom-call(bf16[512,4096]{1,0:T(8,128)(2,1)} %c_hbm.3), custom_call_target="tpu_custom_call" | custom-call | tf_op jit(solution)/shard_map/first_rows/pallas_call | solution.py:95
  1.4 0.5 %collective-permute-start.1 = (bf16[256,2048]{1,0:T(8,128)(2,1)S(1)}, bf16[256,2048]{1,0:T(8,128)(2,1)S(1)}, u32[]{:S(2)}, u32[]{:S(2)}) collective-permute-start(bf16[256,2048]{1,0:T(8,128)(2,1)S(1)} %first_rows.1.sent), channel_id=1, source_target_pairs={{0,1},{1,0},{2,3},{3,2},{4,5},{5,4},{6,7},{7,6},{8,9},{9,8},{10,11... | collective-permute-start | bytes 3145736 | tf_op jit(solution)/shard_map/ppermute | solution.py:189
  1.9 2.2 %load.1 = (bf16[512,2048]{1,0:T(8,128)(2,1)S(1)}, bf16[512,2048]{1,0:T(8,128)(2,1)S(1)}, bf16[256,2048]{1,0:T(8,128)(2,1)S(1)}) custom-call(bf16[512,4096]{1,0:T(8,128)(2,1)} %c_hbm.3, bf16[256,2048]{1,0:T(8,128)(2,1)S(1)} %first_rows.1.sent), custom_call_target="tpu_custom_call" | custom-call | bytes 4194304 | tf_op jit(solution)/shard_map/load/pallas_call | solution.py:109
  4.1 0.2 collective-permute-start
  4.3 0.0 collective-permute-done.1.far_ref
  4.3 8.9 %weights.3 = (f32[16,1024]{1,0:T(8,128)S(1)}, f32[16,1024]{1,0:T(8,128)S(1)}) custom-call(bf16[16,256,512]{2,1,0:T(8,128)(2,1)S(1)} %copy-done, bf16[512,2048]{1,0:T(8,128)(2,1)S(1)} %get-tuple-element.17.c_ref, bf16[256,2048]{1,0:T(8,128)(2,1)S(1)} %collective-permute-done.1.far_ref), custom_call_target="tpu_custom_call" | custom-call | flops 8589934592 | tf_op jit(solution)/shard_map/weights/pallas_call | solution.py:123
  13.3 0.4 collective-permute-start.2
  13.7 0.1 collective-permute-start.3
  13.9 9.1 %weights.2 = (f32[16,1024]{1,0:T(8,128)S(1)}, f32[16,1024]{1,0:T(8,128)S(1)}) custom-call(bf16[16,256,512]{2,1,0:T(8,128)(2,1)S(1)} %copy-done, bf16[512,2048]{1,0:T(8,128)(2,1)S(1)} %get-tuple-element.14.c_ref, bf16[256,2048]{1,0:T(8,128)(2,1)S(1)} %collective-permute-done.far_ref), custom_call_target="tpu_custom_call" | custom-call | flops 8589934592 | tf_op jit(solution)/shard_map/weights/pallas_call | solution.py:123
  23.0 0.0 collective-permute-done.3
  23.0 3.0 %collective-permute-start.7 = (f32[16,1024]{1,0:T(8,128)S(1)}, f32[16,1024]{1,0:T(8,128)S(1)}, u32[]{:S(2)}, u32[]{:S(2)}) collective-permute-start(f32[16,1024]{1,0:T(8,128)S(1)} %add.26), channel_id=1, source_target_pairs={{0,4},{4,0},{8,12},{12,8},{1,5},{5,1},{9,13},{13,9},{2,6},{6,2},{1... | collective-permute-start | bytes 196616 | tf_op jit(solution)/shard_map/ppermute | solution.py:193
  26.0 2.6 %collective-permute-start.4 = (f32[16,1024]{1,0:T(8,128)S(1)}, f32[16,1024]{1,0:T(8,128)S(1)}, u32[]{:S(2)}, u32[]{:S(2)}) collective-permute-start(f32[16,1024]{1,0:T(8,128)S(1)} %add.26), channel_id=1, source_target_pairs={{0,8},{4,12},{8,0},{12,4},{1,9},{5,13},{9,1},{13,5},{2,10},{6,14},... | collective-permute-start | bytes 196616 | tf_op jit(solution)/shard_map/ppermute | solution.py:193
  28.6 0.9 %collective-permute-start.5 = (f32[16,1024]{1,0:T(8,128)S(1)}, f32[16,1024]{1,0:T(8,128)S(1)}, u32[]{:S(2)}, u32[]{:S(2)}) collective-permute-start(f32[16,1024]{1,0:T(8,128)S(1)} %add.27), channel_id=1, source_target_pairs={{0,4},{4,0},{8,12},{12,8},{1,5},{5,1},{9,13},{13,9},{2,6},{6,2},{1... | collective-permute-start | bytes 196616 | tf_op jit(solution)/shard_map/ppermute | solution.py:193
  29.5 3.6 %collective-permute-start.8 = (f32[16,1024]{1,0:T(8,128)S(1)}, f32[16,1024]{1,0:T(8,128)S(1)}, u32[]{:S(2)}, u32[]{:S(2)}) collective-permute-start(f32[16,1024]{1,0:T(8,128)S(1)} %add.31), channel_id=1, source_target_pairs={{0,8},{4,12},{8,0},{12,4},{1,9},{5,13},{9,1},{13,5},{2,10},{6,14},... | collective-permute-start | bytes 196616 | tf_op jit(solution)/shard_map/ppermute | solution.py:193
  33.1 0.5 %collective-permute-done.4 = f32[16,1024]{1,0:T(8,128)S(1)} collective-permute-done((f32[16,1024]{1,0:T(8,128)S(1)}, f32[16,1024]{1,0:T(8,128)S(1)}, u32[]{:S(2)}, u32[]{:S(2)}) %collective-permute-start.4) | collective-permute-done | bytes 65568 | tf_op jit(solution)/shard_map/ppermute | solution.py:193
  33.6 1.9 %collective-permute-done.6 = f32[16,1024]{1,0:T(8,128)S(1)} collective-permute-done((f32[16,1024]{1,0:T(8,128)S(1)}, f32[16,1024]{1,0:T(8,128)S(1)}, u32[]{:S(2)}, u32[]{:S(2)}) %collective-permute-start.6) | collective-permute-done | bytes 65568 | tf_op jit(solution)/shard_map/ppermute | solution.py:193
  35.5 0.0 collective-permute-done.5
  35.5 1.6 %collective-permute-start.11 = (f32[16,1024]{1,0:T(8,128)S(1)}, f32[16,1024]{1,0:T(8,128)S(1)}, u32[]{:S(2)}, u32[]{:S(2)}) collective-permute-start(f32[16,1024]{1,0:T(8,128)S(1)} %add_add_fusion.refs_0_), channel_id=1, source_target_pairs={{0,2},{2,0},{1,3},{3,1},{4,6},{6,4},{5,7},{7,5},{8,10},{10,8},{9,1... | collective-permute-start | bytes 196616 | tf_op jit(solution)/shard_map/ppermute | solution.py:227
  37.1 0.0 collective-permute-start.9
  37.1 0.8 %collective-permute-done.8 = f32[16,1024]{1,0:T(8,128)S(1)} collective-permute-done((f32[16,1024]{1,0:T(8,128)S(1)}, f32[16,1024]{1,0:T(8,128)S(1)}, u32[]{:S(2)}, u32[]{:S(2)}) %collective-permute-start.8) | collective-permute-done | bytes 65568 | tf_op jit(solution)/shard_map/ppermute | solution.py:193
  37.9 0.1 collective-permute-start.10
  38.0 1.9 %collective-permute-done.11 = f32[16,1024]{1,0:T(8,128)S(1)} collective-permute-done((f32[16,1024]{1,0:T(8,128)S(1)}, f32[16,1024]{1,0:T(8,128)S(1)}, u32[]{:S(2)}, u32[]{:S(2)}) %collective-permute-start.11) | collective-permute-done | bytes 65568 | tf_op jit(solution)/shard_map/ppermute | solution.py:227
  39.9 0.0 collective-permute-done.10.refs_3_
  39.9 6.4 %outer.1 = f32[4096,1024]{1,0:T(8,128)} custom-call(f32[16,1024]{1,0:T(8,128)S(1)} %add_add_fusion.refs_0_, f32[16,1024]{1,0:T(8,128)S(1)} %add.32.refs_1_, f32[16,1024]{1,0:T(8,128)S(1)} %collective-permute-done.9.refs_2_, f32[16,1024]{1,0:T(8,128)S(1)} %collective-permute-done.10.refs_3_, f32[16,1024]{1,0:T(8,128)S(1)} %broadcast_select_fusion.refs_4_), custom_call_target="tpu_custom_call" | custom-call | flops 805306368 | bytes 16777216 | tf_op jit(solution)/shard_map/outer/pallas_call | solution.py:174
  (13 shorter events, 0.1 us)
Async XLA Ops:
  0.0 4.3 %copy-start = (bf16[16,256,512]{2,1,0:T(8,128)(2,1)S(1)}, bf16[16,256,512]{2,1,0:T(8,128)(2,1)}, u32[]{:S(2)}) copy-start(bf16[16,256,512]{2,1,0:T(8,128)(2,1)} %d_ref.3) | copy-start | bytes 12582916
  1.4 3.0 %collective-permute-start.1 = (bf16[256,2048]{1,0:T(8,128)(2,1)S(1)}, bf16[256,2048]{1,0:T(8,128)(2,1)S(1)}, u32[]{:S(2)}, u32[]{:S(2)}) collective-permute-start(bf16[256,2048]{1,0:T(8,128)(2,1)S(1)} %first_rows.1.sent), channel_id=1, source_target_pairs={{0,1},{1,0},{2,3},{3,2},{4,5},{5,4},{6,7},{7,6},{8,9},{9,8},{10,11... | collective-permute-start | bytes 3145736 | tf_op jit(solution)/shard_map/ppermute | solution.py:189
  4.1 9.7 %collective-permute-start = (bf16[256,2048]{1,0:T(8,128)(2,1)S(1)}, bf16[256,2048]{1,0:T(8,128)(2,1)S(1)}, u32[]{:S(2)}, u32[]{:S(2)}) collective-permute-start(bf16[256,2048]{1,0:T(8,128)(2,1)S(1)} %get-tuple-element.15), channel_id=1, source_target_pairs={{0,1},{1,0},{2,3},{3,2},{4,5},{5,4},{6,7},{7,6},{8,9},{9,8},{10,11... | collective-permute-start | bytes 3145736 | tf_op jit(solution)/shard_map/ppermute | solution.py:189
  13.3 9.7 %collective-permute-start.2 = (f32[16,1024]{1,0:T(8,128)S(1)}, f32[16,1024]{1,0:T(8,128)S(1)}, u32[]{:S(2)}, u32[]{:S(2)}) collective-permute-start(f32[16,1024]{1,0:T(8,128)S(1)} %get-tuple-element.18), channel_id=1, source_target_pairs={{0,1},{1,0},{2,3},{3,2},{4,5},{5,4},{6,7},{7,6},{8,9},{9,8},{10,11... | collective-permute-start | bytes 196616 | tf_op jit(solution)/shard_map/ppermute | solution.py:189
  13.7 9.3 %collective-permute-start.3 = (f32[16,1024]{1,0:T(8,128)S(1)}, f32[16,1024]{1,0:T(8,128)S(1)}, u32[]{:S(2)}, u32[]{:S(2)}) collective-permute-start(f32[16,1024]{1,0:T(8,128)S(1)} %get-tuple-element.20), channel_id=1, source_target_pairs={{0,1},{1,0},{2,3},{3,2},{4,5},{5,4},{6,7},{7,6},{8,9},{9,8},{10,11... | collective-permute-start | bytes 196616 | tf_op jit(solution)/shard_map/ppermute | solution.py:189
  23.0 6.5 %collective-permute-start.7 = (f32[16,1024]{1,0:T(8,128)S(1)}, f32[16,1024]{1,0:T(8,128)S(1)}, u32[]{:S(2)}, u32[]{:S(2)}) collective-permute-start(f32[16,1024]{1,0:T(8,128)S(1)} %add.26), channel_id=1, source_target_pairs={{0,4},{4,0},{8,12},{12,8},{1,5},{5,1},{9,13},{13,9},{2,6},{6,2},{1... | collective-permute-start | bytes 196616 | tf_op jit(solution)/shard_map/ppermute | solution.py:193
  26.0 7.5 %collective-permute-start.4 = (f32[16,1024]{1,0:T(8,128)S(1)}, f32[16,1024]{1,0:T(8,128)S(1)}, u32[]{:S(2)}, u32[]{:S(2)}) collective-permute-start(f32[16,1024]{1,0:T(8,128)S(1)} %add.26), channel_id=1, source_target_pairs={{0,8},{4,12},{8,0},{12,4},{1,9},{5,13},{9,1},{13,5},{2,10},{6,14},... | collective-permute-start | bytes 196616 | tf_op jit(solution)/shard_map/ppermute | solution.py:193
  28.6 6.9 %collective-permute-start.6 = (f32[16,1024]{1,0:T(8,128)S(1)}, f32[16,1024]{1,0:T(8,128)S(1)}, u32[]{:S(2)}, u32[]{:S(2)}) collective-permute-start(f32[16,1024]{1,0:T(8,128)S(1)} %add.27), channel_id=1, source_target_pairs={{0,12},{4,8},{8,4},{12,0},{1,13},{5,9},{9,5},{13,1},{2,14},{6,10},... | collective-permute-start | bytes 196616 | tf_op jit(solution)/shard_map/ppermute | solution.py:193
  28.6 6.9 %collective-permute-start.5 = (f32[16,1024]{1,0:T(8,128)S(1)}, f32[16,1024]{1,0:T(8,128)S(1)}, u32[]{:S(2)}, u32[]{:S(2)}) collective-permute-start(f32[16,1024]{1,0:T(8,128)S(1)} %add.27), channel_id=1, source_target_pairs={{0,4},{4,0},{8,12},{12,8},{1,5},{5,1},{9,13},{13,9},{2,6},{6,2},{1... | collective-permute-start | bytes 196616 | tf_op jit(solution)/shard_map/ppermute | solution.py:193
  29.5 8.3 %collective-permute-start.8 = (f32[16,1024]{1,0:T(8,128)S(1)}, f32[16,1024]{1,0:T(8,128)S(1)}, u32[]{:S(2)}, u32[]{:S(2)}) collective-permute-start(f32[16,1024]{1,0:T(8,128)S(1)} %add.31), channel_id=1, source_target_pairs={{0,8},{4,12},{8,0},{12,4},{1,9},{5,13},{9,1},{13,5},{2,10},{6,14},... | collective-permute-start | bytes 196616 | tf_op jit(solution)/shard_map/ppermute | solution.py:193
  35.5 4.3 %collective-permute-start.11 = (f32[16,1024]{1,0:T(8,128)S(1)}, f32[16,1024]{1,0:T(8,128)S(1)}, u32[]{:S(2)}, u32[]{:S(2)}) collective-permute-start(f32[16,1024]{1,0:T(8,128)S(1)} %add_add_fusion.refs_0_), channel_id=1, source_target_pairs={{0,2},{2,0},{1,3},{3,1},{4,6},{6,4},{5,7},{7,5},{8,10},{10,8},{9,1... | collective-permute-start | bytes 196616 | tf_op jit(solution)/shard_map/ppermute | solution.py:227
  37.1 2.8 %collective-permute-start.9 = (f32[16,1024]{1,0:T(8,128)S(1)}, f32[16,1024]{1,0:T(8,128)S(1)}, u32[]{:S(2)}, u32[]{:S(2)}) collective-permute-start(f32[16,1024]{1,0:T(8,128)S(1)} %add_add_fusion.refs_0_), channel_id=1, source_target_pairs={{0,1},{1,0},{2,3},{3,2},{4,5},{5,4},{6,7},{7,6},{8,9},{9,8},{10,11... | collective-permute-start | bytes 196616 | tf_op jit(solution)/shard_map/ppermute | solution.py:189
  37.9 2.0 %collective-permute-start.10 = (f32[16,1024]{1,0:T(8,128)S(1)}, f32[16,1024]{1,0:T(8,128)S(1)}, u32[]{:S(2)}, u32[]{:S(2)}) collective-permute-start(f32[16,1024]{1,0:T(8,128)S(1)} %add.32.refs_1_), channel_id=1, source_target_pairs={{0,1},{1,0},{2,3},{3,2},{4,5},{5,4},{6,7},{7,6},{8,9},{9,8},{10,11... | collective-permute-start | bytes 196616 | tf_op jit(solution)/shard_map/ppermute | solution.py:189
